TPU v7x, 32 devices: a whole 2x2x4 slice. The times are simulated.
32 devices in a mesh: mp: 4 (over y, core), replica: 8 (over z, x).
Axes of the slice: x: 2, y: 2, z: 4, core: 2. Of those that a mesh axis runs over, the one named last changes fastest.
Arguments:
- weight: float32 [2560, 5120], P('mp'), may hold values from -6 to 6
- first_moment: bfloat16 [8, 2560, 5120], P('replica', 'mp'), may hold values from -0.0011978149 to 0.0011978149
- second_moment: bfloat16 [8, 2560, 5120], P('replica', 'mp'), may hold values from 9.95351e-09 to 9.983778e-07
- outer_momentum: float32 [2560, 5120], P(('mp', 'replica')), may hold values from -0.3 to 0.3
- act_table: bfloat16 [2048, 5120], P(None, 'mp'), may hold values from -6 to 6
- token_ids: int32 [8, 2, 512], P('replica'), may hold values from 0 to 2047
- targets: bfloat16 [8, 2, 512, 2560], P('replica', None, None, 'mp'), may hold values from -6 to 6
Outputs:
- new_weight: float32 [2560, 5120], P('mp')
- momentum: float32 [2560, 5120], P(('mp', 'replica'))
All inputs are finite; a program needn't handle non-finite values. Where the computation divides by a largest or mean magnitude, that divisor is 1e-20 or more.
Results may differ from a plain program's by a relative error of at most 0.002.
Values may be sent and summed in bfloat16 or wider, within the bound.
A program may use at most 128 MiB of HBM per device.

v0:
```python
import jax
import jax.numpy as jnp
from jax import lax
from jax.sharding import PartitionSpec as P

STEPS = 2
BLOCK = 128
PRIOR_STEPS = 3


beta_first = 0.9
beta_second = 0.95
adam_epsilon = 1e-08
inner_rate = 0.1
weight_decay = 0.1
outer_mu = 0.9
outer_rate = 0.7
scale_epsilon = 1e-06


def encode(values):
    row_count = values.shape[0]
    blocks = values.reshape(row_count, -1, BLOCK)
    scales = (jnp.max(jnp.abs(blocks), axis=2) + scale_epsilon).astype(jnp.bfloat16)
    code_values = (blocks / scales.astype(jnp.float32)[:, :, None]).astype(jnp.bfloat16)
    return (code_values.reshape(row_count, -1), scales)


def decode(code_values, scales):
    row_count = code_values.shape[0]
    blocks = code_values.astype(jnp.float32).reshape(row_count, scales.shape[1], -1)
    return (blocks * scales.astype(jnp.float32)[:, :, None]).reshape(row_count, -1)


def shards(weight, first_moment, second_moment, outer_momentum, act_table, token_ids, targets):
    row_count, width = weight.shape
    tokens_step = token_ids.shape[2]
    factor = width ** (-0.5)
    current = weight
    moment_one = first_moment[0].astype(jnp.float32)
    moment_two = second_moment[0].astype(jnp.float32)
    for inner_step in range(STEPS):
        local_inputs = jnp.take(act_table, token_ids[0, inner_step], axis=0)
        weight_half = current.astype(jnp.bfloat16)
        wanted = targets[0, inner_step].astype(jnp.float32)
        inputs = lax.all_gather(local_inputs, "mp", axis=1, tiled=True)
        output = (
            lax.dot_general(
                inputs, weight_half, (((1,), (1,)), ((), ())), preferred_element_type=jnp.float32
            )
            * factor
        )
        signal = (output - wanted).astype(jnp.bfloat16)
        gradient = lax.dot_general(
            signal, inputs, (((0,), (0,)), ((), ())), preferred_element_type=jnp.float32
        ) * (factor / tokens_step)
        step_count = PRIOR_STEPS + inner_step + 1
        moment_one = beta_first * moment_one + (1.0 - beta_first) * gradient
        moment_two = beta_second * moment_two + (1.0 - beta_second) * gradient * gradient
        update = (
            moment_one
            / (1.0 - beta_first**step_count)
            / (jnp.sqrt(moment_two / (1.0 - beta_second**step_count)) + adam_epsilon)
        )
        current = current - inner_rate * (update + weight_decay * current)
    delta = weight - current
    code_values, scales = encode(delta)
    replicas = lax.axis_size("replica")
    fragment = row_count // replicas
    blocks_row = scales.shape[1]
    got_codes, got_scales = (
        lax.all_to_all(
            code_values.reshape(replicas, fragment, width),
            "replica",
            split_axis=0,
            concat_axis=0,
            tiled=True,
        ),
        lax.all_to_all(
            scales.reshape(replicas, fragment, blocks_row),
            "replica",
            split_axis=0,
            concat_axis=0,
            tiled=True,
        ),
    )
    decoded = decode(
        got_codes.reshape(replicas * fragment, width),
        got_scales.reshape(replicas * fragment, blocks_row),
    )
    summed = jnp.sum(decoded.reshape(replicas, fragment, width), axis=0)
    average = summed / replicas
    momentum = outer_mu * outer_momentum + average
    outer_update = average + outer_mu * momentum
    update_codes, update_scales = encode(outer_update)
    all_codes, all_scales = (
        lax.all_gather(update_codes, "replica", axis=0, tiled=True),
        lax.all_gather(update_scales, "replica", axis=0, tiled=True),
    )
    new_weight = weight - outer_rate * decode(all_codes, all_scales)
    return (new_weight, momentum)


def solution(mesh):
    in_specs = (
        P("mp", None),
        P("replica", "mp", None),
        P("replica", "mp", None),
        P(("mp", "replica"), None),
        P(None, "mp"),
        P("replica", None, None),
        P("replica", None, None, "mp"),
    )
    out_specs = (P("mp", None), P(("mp", "replica"), None))
    return jax.shard_map(shards, mesh=mesh, in_specs=in_specs, out_specs=out_specs, check_vma=False)
```

profile of v0, /device:TPU:0, one launch (start us, length us, event | category | flops | bytes accessed | tf_op | source)
XLA Modules:
  0.0 507.6 jit_solution(12050893851079680873)
XLA Ops:
  7.2 0.0 all-gather.5.cloned.1.call-start
  7.2 0.8 fusion.27
  8.0 0.0 copy-start.2
  8.0 6.4 %gather_fusion = bf16[512,1280]{1,0:T(8,128)(2,1)S(1)} fusion(bf16[2048,1280]{1,0:T(8,128)(2,1)} %param.13, s32[1024]{0:T(1024)S(1)} %pad_clamp_fusion.1), kind=kCustom, calls=%fused_computation.clone | custom fusion | bytes 2623488 | tf_op jit(solution)/shard_map/jit(_take)/gather | solution.py:43
  14.4 1.2 broadcast_select_fusion.1
  15.7 0.0 all-gather.5.cloned.1.call-update
  15.7 0.0 all-gather.7.cloned.1.call-start
  15.8 6.3 %gather_fusion.1 = bf16[512,1280]{1,0:T(8,128)(2,1)S(1)} fusion(bf16[2048,1280]{1,0:T(8,128)(2,1)} %param.13, s32[1024]{0:T(1024)S(1)} %pad_clamp_fusion), kind=kCustom, calls=%fused_computation.1.clone | custom fusion | bytes 2623488 | tf_op jit(solution)/shard_map/jit(_take)/gather | solution.py:43
  22.1 1.3 broadcast_select_fusion
  23.3 0.0 all-gather.7.cloned.1.call-update
  23.4 35.6 %all-gather.5.cloned.1.call-done = bf16[512,5120]{1,0:T(8,128)(2,1)} async-done(((bf16[512,1280]{1,0:T(8,128)(2,1)}), bf16[512,5120]{1,0:T(8,128)(2,1)}) %all-gather.5.cloned.1.call-update) | async-done | bytes 5242896 | tf_op jit(solution)/shard_map/all_gather | solution.py:46
  59.0 0.0 copy-done.2
  59.0 0.0 copy-start.1
  59.0 10.7 %fusion.19 = bf16[512,640]{1,0:T(8,128)(2,1)S(1)} fusion(bf16[512,5120]{1,0:T(8,128)(2,1)} %all-gather.5.cloned.1.call-done, f32[640,5120]{1,0:T(8,128)} %param.9, bf16[1,2,512,640]{3,2,1,0:T(8,128)(2,1)S(1)} %copy-done.2), kind=kOutput, calls=%fused_computation.25 | convolution fusion | flops 3360030720 | bytes 19660800 | tf_op jit(solution)/shard_map/dot_general | solution.py:48
  69.7 0.0 copy-done.1
  69.7 6.9 %fusion.28 = f32[640,5120]{1,0:T(8,128)} fusion(bf16[512,640]{1,0:T(8,128)(2,1)S(1)} %fusion.19, bf16[512,5120]{1,0:T(8,128)(2,1)S(1)} %copy-done.1), kind=kOutput, calls=%fused_computation.40 | convolution fusion | flops 3355443200 | bytes 19005440 | tf_op jit(solution)/shard_map/dot_general | solution.py:54
  76.6 24.4 %all-gather.7.cloned.1.call-done = bf16[512,5120]{1,0:T(8,128)(2,1)} async-done(((bf16[512,1280]{1,0:T(8,128)(2,1)}), bf16[512,5120]{1,0:T(8,128)(2,1)}) %all-gather.7.cloned.1.call-update) | async-done | bytes 5242896 | tf_op jit(solution)/shard_map/all_gather | solution.py:46
  101.0 20.9 %fusion.22 = bf16[512,640]{1,0:T(8,128)(2,1)S(1)} fusion(bf16[512,5120]{1,0:T(8,128)(2,1)} %all-gather.7.cloned.1.call-done, bf16[1,2,512,640]{3,2,1,0:T(8,128)(2,1)S(1)} %copy-done.2, f32[640,5120]{1,0:T(8,128)} %param.9, f32[640,5120]{1,0:T(8,128)} %fusion.28, bf16[1,640,5120]{2,1,0:T(8,128)(2,1)} %param.10, bf16[1,640,5120]{2,1,0:T(8,128)(2,1)} %param.11), kind=kOutput, calls=%fused_computation.26 | convolution fusion | flops 3419013120 | bytes 45875200 | tf_op jit(solution)/shard_map/dot_general | solution.py:48
  121.9 34.5 %abs_bitcast_fusion = (f32[80,8,40,128]{3,1,2,0:T(8,128)}, f32[640,5120]{1,0:T(8,128)}) fusion(f32[640,5120]{1,0:T(8,128)} %param.9, f32[640,5120]{1,0:T(8,128)} %fusion.28, bf16[1,640,5120]{2,1,0:T(8,128)(2,1)} %param.11, bf16[1,640,5120]{2,1,0:T(8,128)(2,1)} %param.10, bf16[512,640]{1,0:T(8,128)(2,1)S(1)} %fusion.22, ...), kind=kOutput, calls=%fused_computation.9 | convolution fusion | flops 3473408000 | bytes 71434240 | tf_op jit(solution)/shard_map/dot_general | solution.py:54
  156.4 12.4 %copy.36 = f32[80,8,40,128]{3,2,1,0:T(8,128)} copy(f32[80,8,40,128]{3,1,2,0:T(8,128)} %get-tuple-element.5) | data formatting | bytes 26214400
  168.8 8.2 %reduce_max.18 = f32[640,40]{1,0:T(8,128)S(1)} reduce(f32[640,40,128]{2,1,0:T(8,128)} %bitcast.64, f32[]{:T(128)} %constant.49.clone.1), dimensions={2}, to_apply=%region_0.0 | reduce | flops 3251200 | bytes 13209604 | tf_op jit(solution)/shard_map/reduce_max | solution.py:24
  177.0 0.1 copy.24
  177.2 0.1 copy.25
  177.3 0.1 convert_element_type.107
  177.4 7.3 %div.68 = f32[640,40,128]{2,1,0:T(8,128)} broadcast(f32[640,40]{1,0:T(8,128)S(1)} %copy.25), dimensions={0,1} | broadcast | bytes 13209600 | tf_op jit(solution)/shard_map/div | solution.py:25
  184.8 14.3 %div.69 = f32[8,80,5120]{2,1,0:T(8,128)} reshape(f32[640,40,128]{2,1,0:T(8,128)} %div.68) | data formatting | bytes 26214400 | tf_op jit(solution)/shard_map/div | solution.py:25
  199.0 0.6 copy.26
  199.7 5.5 %all-to-all-start.1 = ((bf16[8,80,40]{1,2,0:T(8,128)(2,1)}), bf16[8,80,40]{1,2,0:T(8,128)(2,1)S(1)}, u32[]{:S(2)}, u32[]{:S(2)}) async-start(bf16[8,80,40]{1,2,0:T(8,128)(2,1)} %copy.26), calls=%async_computation.1 | async-start | bytes 163840 | tf_op jit(solution)/shard_map/all_to_all | solution.py:79
  205.2 12.1 %divide_convert_fusion = bf16[8,80,5120]{2,1,0:T(8,128)(2,1)} fusion(f32[8,80,5120]{2,1,0:T(8,128)} %bitcast.65, f32[8,80,5120]{2,1,0:T(8,128)} %div.69), kind=kLoop, calls=%fused_computation.8 | loop fusion | flops 6553600 | bytes 32768000 | tf_op jit(solution)/shard_map/convert_element_type | solution.py:25
  217.2 0.0 all-to-all-done.1
  217.2 6.0 %all-to-all-start = ((bf16[8,80,5120]{2,1,0:T(8,128)(2,1)}), bf16[8,80,5120]{2,1,0:T(8,128)(2,1)}, u32[]{:S(2)}, u32[]{:S(2)}) async-start(bf16[8,80,5120]{2,1,0:T(8,128)(2,1)} %divide_convert_fusion), calls=%async_computation | async-start | bytes 13107200 | tf_op jit(solution)/shard_map/all_to_all | solution.py:72
  223.2 0.0 all-gather.9.cloned.1.call-start
  223.3 0.1 copy.32
  223.4 7.4 %mul.120 = f32[640,40,128]{2,1,0:T(8,128)} broadcast(f32[640,40]{1,0:T(8,128)S(1)} %bitcast.71), dimensions={0,1} | broadcast | bytes 13209600 | tf_op jit(solution)/shard_map/mul | solution.py:32
  230.8 14.3 %mul.121 = f32[8,80,5120]{2,1,0:T(8,128)} reshape(f32[640,40,128]{2,1,0:T(8,128)} %mul.120) | data formatting | bytes 26214400 | tf_op jit(solution)/shard_map/mul | solution.py:32
  245.1 121.8 %all-to-all-done = bf16[8,80,5120]{2,1,0:T(8,128)(2,1)} async-done(((bf16[8,80,5120]{2,1,0:T(8,128)(2,1)}), bf16[8,80,5120]{2,1,0:T(8,128)(2,1)}, u32[]{:S(2)}, u32[]{:S(2)}) %all-to-all-start) | async-done | bytes 6553632 | tf_op jit(solution)/shard_map/all_to_all | solution.py:72
  367.0 8.7 %multiply_reduce_fusion = f32[80,5120]{1,0:T(8,128)S(1)} fusion(f32[8,80,5120]{2,1,0:T(8,128)} %mul.121, bf16[8,80,5120]{2,1,0:T(8,128)(2,1)} %all-to-all-done), kind=kLoop, calls=%fused_computation.7 | loop fusion | flops 9420800 | bytes 21299200 | tf_op jit(solution)/shard_map/reduce_sum | solution.py:91
  375.7 1.8 abs_bitcast_fusion.1
  377.5 0.0 copy-start
  377.6 1.7 copy.37
  379.2 1.9 reduce_max.19
  381.2 0.5 div.73
  381.6 1.4 fusion.6
  383.0 0.0 all-gather.9.cloned.1.call-update
  383.1 0.1 copy.29
  383.2 31.3 %all-gather = bf16[8,80,40]{1,2,0:T(8,128)(2,1)S(1)} all-gather(bf16[1,80,40]{1,2,0:T(8,128)(2,1)S(1)} %copy.29), channel_id=1, replica_groups=mesh['mp'=4,'replica'=8] {'replica'}, dimensions={0}, use_global_device_ids=true | all-gather | bytes 57600 | tf_op jit(solution)/shard_map/all_gather | solution.py:98
  414.4 0.1 copy.33
  414.5 69.7 %all-gather.9.cloned.1.call-done = bf16[640,5120]{1,0:T(8,128)(2,1)} async-done(((bf16[80,5120]{1,0:T(8,128)(2,1)}), bf16[640,5120]{1,0:T(8,128)(2,1)}) %all-gather.9.cloned.1.call-update) | async-done | bytes 6553616 | tf_op jit(solution)/shard_map/all_gather | solution.py:97
  484.2 0.0 slice-start
  484.2 0.0 slice-start.1
  484.2 3.6 mul.125
  487.9 0.0 copy-done
  487.9 0.0 slice-done
  487.9 0.0 slice-done.1
  487.9 12.8 %fusion.1 = f32[640,5120]{1,0:T(8,128)} fusion(f32[640,5120]{1,0:T(8,128)} %param.9, f32[80,8,40,128]{3,2,1,0:T(8,128)S(1)} %bitcast.63, bf16[640,5120]{1,0:T(8,128)(2,1)S(1)} %bitcast.69), kind=kLoop, calls=%fused_computation.4 | loop fusion | flops 13107200 | bytes 45875200 | tf_op jit(solution)/shard_map/sub | solution.py:100
  (9 shorter events, 0.1 us)
Async XLA Ops:
  7.2 51.8 %all-gather.5.cloned.1.call-start = ((), (), s32[]{:S(2)}) async-start(), calls=%async_computation.2 | async-start | bytes 6553600 | tf_op jit(solution)/shard_map/all_gather | solution.py:46
  8.0 51.0 %copy-start.2 = (bf16[1,2,512,640]{3,2,1,0:T(8,128)(2,1)S(1)}, bf16[1,2,512,640]{3,2,1,0:T(8,128)(2,1)}, u32[]{:S(2)}) copy-start(bf16[1,2,512,640]{3,2,1,0:T(8,128)(2,1)} %param.15) | copy-start | bytes 3932164
  15.7 85.3 %all-gather.7.cloned.1.call-start = ((), (), s32[]{:S(2)}) async-start(), calls=%async_computation.3 | async-start | bytes 6553600 | tf_op jit(solution)/shard_map/all_gather | solution.py:46
  59.0 10.7 %copy-start.1 = (bf16[512,5120]{1,0:T(8,128)(2,1)S(1)}, bf16[512,5120]{1,0:T(8,128)(2,1)}, u32[]{:S(2)}) copy-start(bf16[512,5120]{1,0:T(8,128)(2,1)} %all-gather.5.cloned.1.call-done) | copy-start | bytes 15728644
  199.7 17.6 %all-to-all-start.1 = ((bf16[8,80,40]{1,2,0:T(8,128)(2,1)}), bf16[8,80,40]{1,2,0:T(8,128)(2,1)S(1)}, u32[]{:S(2)}, u32[]{:S(2)}) async-start(bf16[8,80,40]{1,2,0:T(8,128)(2,1)} %copy.26), calls=%async_computation.1 | async-start | bytes 163840 | tf_op jit(solution)/shard_map/all_to_all | solution.py:79
  217.2 149.7 %all-to-all-start = ((bf16[8,80,5120]{2,1,0:T(8,128)(2,1)}), bf16[8,80,5120]{2,1,0:T(8,128)(2,1)}, u32[]{:S(2)}, u32[]{:S(2)}) async-start(bf16[8,80,5120]{2,1,0:T(8,128)(2,1)} %divide_convert_fusion), calls=%async_computation | async-start | bytes 13107200 | tf_op jit(solution)/shard_map/all_to_all | solution.py:72
  223.2 260.9 %all-gather.9.cloned.1.call-start = ((), (), s32[]{:S(2)}) async-start(), calls=%async_computation.4 | async-start | bytes 7372800 | tf_op jit(solution)/shard_map/all_gather | solution.py:97
  377.5 110.3 %copy-start = (f32[80,5120]{1,0:T(8,128)}, f32[80,5120]{1,0:T(8,128)S(1)}, u32[]{:S(2)}) copy-start(f32[80,5120]{1,0:T(8,128)S(1)} %get-tuple-element.4) | copy-start | bytes 4915204
  484.2 3.7 slice-start
  484.2 3.7 slice-start.1
Sparse Core Ops, SparseCore 0:
  15.8 43.1 all-gather.4
  60.5 40.4 all-gather.6
  383.2 100.9 all-gather.8
where the time goes:
time: 516 us; the launch traced here: 508 us
  waiting for transfers between devices  252 us (49%)
  local copies, waits for them, and re-layouts  76.3 us (15%)
  matrix products  73 us (14%)
  other arithmetic  49.5 us (10%)
  blocking collectives  31.3 us (6%)
  between operations  14.4 us (3%)
  starting transfers between devices  11.6 us (2%)
    all_to_all x1, waiting for transfers between devices, shards(): lax.all_to_all(code_values.reshape(replicas, fragment, width), 'replica',...  122 us
    all_gather x1, waiting for transfers between devices, shards(): lax.all_gather(update_codes, 'replica', axis=0, tiled=True)  69.7 us
    all_gather x2, waiting for transfers between devices, shards(): inputs = lax.all_gather(local_inputs, 'mp', axis=1, tiled=True)  60 us
    dot_general x2, matrix products, shards(): lax.dot_general(signal, inputs, (((0,), (0,)), ((), ())), preferred_eleme...  41.4 us
    dot_general x2, matrix products, shards(): lax.dot_general(inputs, weight_half, (((1,), (1,)), ((), ())), preferred_...  31.6 us
    all_gather x1, blocking collectives, shards(): lax.all_gather(update_scales, 'replica', axis=0, tiled=True)  31.3 us
    mul x3, local copies, waits for them, and re-layouts, decode(): blocks * scales.astype(jnp.float32)[:, :, None]  25.3 us
    div x3, local copies, waits for them, and re-layouts, encode(): blocks / scales.astype(jnp.float32)[:, :, None]  22.1 us
  transfers between devices with their start and end apart: 5, of which 4 were waited for; matrix products, arithmetic and copies ran while one was open for 12% of the time, Pallas kernels for 0%

commit v1 on v0

--- a/solution.py
+++ b/solution.py
@@ -1,6 +1,10 @@
+import functools
+
 import jax
 import jax.numpy as jnp
 from jax import lax
+from jax.experimental import pallas as pl
+from jax.experimental.pallas import tpu as pltpu
 from jax.sharding import PartitionSpec as P
 
 STEPS = 2
@@ -32,7 +36,7 @@
     return (blocks * scales.astype(jnp.float32)[:, :, None]).reshape(row_count, -1)
 
 
-def shards(weight, first_moment, second_moment, outer_momentum, act_table, token_ids, targets):
+def shards_plain(weight, first_moment, second_moment, outer_momentum, act_table, token_ids, targets):
     row_count, width = weight.shape
     tokens_step = token_ids.shape[2]
     factor = width ** (-0.5)
@@ -101,6 +105,313 @@
     return (new_weight, momentum)
 
 
+MESH = pl.DeviceIdType.MESH
+TILE = 16
+
+
+def adam(current, moment_one, moment_two, gradient, unit, step_count):
+    one = beta_first * moment_one + ((1.0 - beta_first) * unit) * gradient
+    two = beta_second * moment_two + ((1.0 - beta_second) * unit * unit) * (gradient * gradient)
+    spread = two * (1.0 / (1.0 - beta_second**step_count))
+    bottom = spread * lax.rsqrt(spread) + adam_epsilon
+    update = (one * (inner_rate / (1.0 - beta_first**step_count))) / bottom
+    return (1.0 - inner_rate * weight_decay) * current - update, one, two
+
+
+def inner_kernel(
+    chunks, factor, unit, x1, x2, w, m, v, t1, t2, codes, scales, acc, s1, s2, g1, g2, half, all_scales
+):
+    phase, chunk = pl.program_id(0), pl.program_id(1)
+    row_count, wide = w.shape
+    rows_of = lambda i: pl.ds(pl.multiple_of(i * TILE, TILE), TILE)
+
+    def add_output(weights, inputs, wanted, signal):
+        part = lax.dot_general(
+            weights, inputs, (((1,), (1,)), ((), ())), preferred_element_type=jnp.float32
+        )
+
+        @pl.when(chunk == 0)
+        def _():
+            acc[...] = part
+
+        @pl.when(chunk > 0)
+        def _():
+            acc[...] += part
+
+        @pl.when(chunk == chunks - 1)
+        def _():
+            signal[...] = (acc[...] * factor - wanted[...].astype(jnp.float32)).astype(jnp.bfloat16)
+
+    def first_step(rows):
+        return adam(
+            w[rows, :],
+            m[rows, :].astype(jnp.float32),
+            v[rows, :].astype(jnp.float32),
+            g1[chunk, rows, :],
+            unit,
+            PRIOR_STEPS + 1,
+        )
+
+    @pl.when(phase == 0)
+    def _():
+        add_output(w[...].astype(jnp.bfloat16), x1[...], t1, s1)
+
+    @pl.when(phase == 1)
+    def _():
+        g1[chunk] = jnp.dot(s1[...], x1[...], preferred_element_type=jnp.float32)
+
+        def body(i, carry):
+            half[rows_of(i), :] = first_step(rows_of(i))[0].astype(jnp.bfloat16)
+            return carry
+
+        lax.fori_loop(0, row_count // TILE, body, 0, unroll=2)
+        add_output(half[...], x2[...], t2, s2)
+
+    @pl.when(phase == 2)
+    def _():
+        g2[...] = jnp.dot(s2[...], x2[...], preferred_element_type=jnp.float32)
+        lane = lax.broadcasted_iota(jnp.int32, (TILE, BLOCK), 1)
+
+        @pl.when(chunk == 0)
+        def _():
+            all_scales[...] = jnp.zeros_like(all_scales)
+
+        def body(i, carry):
+            rows = rows_of(i)
+            current, one, two = first_step(rows)
+            current, _, _ = adam(current, one, two, g2[rows, :], unit, PRIOR_STEPS + 2)
+            delta = w[rows, :] - current
+            kept = all_scales[rows, :]
+            for block in range(wide // BLOCK):
+                values = delta[:, block * BLOCK : (block + 1) * BLOCK]
+                largest = jnp.max(jnp.abs(values), axis=1, keepdims=True)
+                scale = (largest + scale_epsilon).astype(jnp.bfloat16).astype(jnp.float32)
+                codes[rows, block * BLOCK : (block + 1) * BLOCK] = (values / scale).astype(jnp.bfloat16)
+                kept = jnp.where(lane == chunk * (wide // BLOCK) + block, scale, kept)
+            all_scales[rows, :] = kept
+            return carry
+
+        lax.fori_loop(0, row_count // TILE, body, 0, unroll=2)
+
+        @pl.when(chunk == chunks - 1)
+        def _():
+            scales[...] = all_scales[...].astype(jnp.bfloat16)
+
+
+def inner_steps(inputs, weight, first, second, wanted):
+    row_count, width = weight.shape
+    tokens = wanted.shape[2]
+    wide = 512 if width % 512 == 0 else BLOCK
+    chunks = width // wide
+    factor = width ** (-0.5)
+    later = lambda phase, chunk: chunk * jnp.minimum(phase, 1)
+    columns = lambda phase, chunk: (0, chunk)
+    whole = lambda phase, chunk: (0, 0)
+    return pl.pallas_call(
+        functools.partial(inner_kernel, chunks, factor, factor / tokens),
+        grid=(3, chunks),
+        out_shape=(
+            jax.ShapeDtypeStruct((row_count, width), jnp.bfloat16),
+            jax.ShapeDtypeStruct((row_count, BLOCK), jnp.bfloat16),
+        ),
+        in_specs=[
+            pl.BlockSpec((tokens, wide), lambda phase, chunk: (0, jnp.where(phase < 2, chunk, chunks - 1))),
+            pl.BlockSpec((tokens, wide), lambda phase, chunk: (1, later(phase, chunk))),
+            pl.BlockSpec((row_count, wide), columns),
+            pl.BlockSpec((row_count, wide), lambda phase, chunk: (0, later(phase, chunk))),
+            pl.BlockSpec((row_count, wide), lambda phase, chunk: (0, later(phase, chunk))),
+            pl.BlockSpec((row_count, tokens), whole),
+            pl.BlockSpec((row_count, tokens), whole),
+        ],
+        out_specs=(
+            pl.BlockSpec((row_count, wide), lambda phase, chunk: (0, chunk * (phase // 2))),
+            pl.BlockSpec((row_count, BLOCK), whole),
+        ),
+        scratch_shapes=[
+            pltpu.VMEM((row_count, tokens), jnp.float32),
+            pltpu.VMEM((row_count, tokens), jnp.bfloat16),
+            pltpu.VMEM((row_count, tokens), jnp.bfloat16),
+            pltpu.VMEM((chunks, row_count, wide), jnp.float32),
+            pltpu.VMEM((row_count, wide), jnp.float32),
+            pltpu.VMEM((row_count, wide), jnp.bfloat16),
+            pltpu.VMEM((row_count, BLOCK), jnp.float32),
+        ],
+        compiler_params=pltpu.CompilerParams(vmem_limit_bytes=48 * 2**20),
+        cost_estimate=pl.CostEstimate(
+            flops=8 * row_count * width * tokens, bytes_accessed=30 * row_count * width, transcendentals=0
+        ),
+    )(inputs, inputs, weight, first, second, wanted[0], wanted[1])
+
+
+def flipped(place, bits):
+    bit = 1
+    while bit <= bits:
+        if bits & bit:
+            place = place + bit * (1 - 2 * lax.rem(place // bit, 2))
+        bit *= 2
+    return place
+
+
+PARTS = 2
+
+
+def exchange_kernel(
+    replicas, codes, scales, outer, momentum, update, got_codes, got_scales, pair_out, pair_in, own,
+    code_send, code_recv, scale_send, scale_recv, pair_send, pair_recv,
+):
+    groups = replicas // 2
+    me = lax.axis_index("replica")
+    group, side = me // 2, lax.rem(me, 2)
+    partner = 2 * group + 1 - side
+    fragment, width = outer.shape
+    wide = width // PARTS
+
+    barrier = pltpu.get_barrier_semaphore()
+    pl.semaphore_signal(barrier, inc=1, device_id={"replica": partner}, device_id_type=MESH)
+    for turn in range(1, groups):
+        pl.semaphore_signal(
+            barrier, inc=1, device_id={"replica": 2 * flipped(group, turn) + side}, device_id_type=MESH
+        )
+    pl.semaphore_wait(barrier, groups)
+
+    order = [(turn, part) for turn in range(groups - 1, -1, -1) for part in range(PARTS)]
+
+    def code_copy(i):
+        turn, part = order[i]
+        columns = pl.ds(part * wide, wide)
+        return pltpu.make_async_remote_copy(
+            src_ref=codes.at[2 * flipped(group, turn) + 1 - side, :, columns],
+            dst_ref=got_codes.at[turn, :, columns],
+            send_sem=code_send.at[i],
+            recv_sem=code_recv.at[i],
+            device_id={"replica": partner},
+            device_id_type=MESH,
+        )
+
+    def scale_copy(turn):
+        return pltpu.make_async_remote_copy(
+            src_ref=scales.at[2 * flipped(group, turn) + 1 - side],
+            dst_ref=got_scales.at[turn],
+            send_sem=scale_send.at[turn],
+            recv_sem=scale_recv.at[turn],
+            device_id={"replica": partner},
+            device_id_type=MESH,
+        )
+
+    def pair_copy(i):
+        turn, part = order[i]
+        columns = pl.ds(part * wide, wide)
+        return pltpu.make_async_remote_copy(
+            src_ref=pair_out.at[turn - 1, :, columns],
+            dst_ref=pair_in.at[turn - 1, :, columns],
+            send_sem=pair_send.at[i],
+            recv_sem=pair_recv.at[i],
+            device_id={"replica": 2 * flipped(group, turn) + side},
+            device_id_type=MESH,
+        )
+
+    for turn in range(groups):
+        scale_copy(turn).start()
+    code_copy(0).start()
+    code_copy(1).start()
+    for i, (turn, part) in enumerate(order):
+        if part == 0:
+            scale_copy(turn).wait()
+        code_copy(i).wait()
+        if i + 2 < len(order):
+            code_copy(i + 2).start()
+        mine = 2 * flipped(group, turn) + side
+
+        def body(step, carry):
+            rows = pl.ds(pl.multiple_of(step * TILE, TILE), TILE)
+            my_scales = scales[mine, rows, :].astype(jnp.float32)
+            their_scales = got_scales[turn, rows, :].astype(jnp.float32)
+            for block in range(wide // BLOCK):
+                at = part * (wide // BLOCK) + block
+                columns = slice(at * BLOCK, (at + 1) * BLOCK)
+                total = (
+                    codes[mine, rows, columns].astype(jnp.float32) * my_scales[:, at : at + 1]
+                    + got_codes[turn, rows, columns].astype(jnp.float32) * their_scales[:, at : at + 1]
+                )
+                if turn:
+                    pair_out[turn - 1, rows, columns] = total.astype(jnp.bfloat16)
+                else:
+                    own[rows, columns] = total
+            return carry
+
+        lax.fori_loop(0, fragment // TILE, body, 0)
+        if turn:
+            pair_copy(i).start()
+    for i, (turn, part) in enumerate(order):
+        if turn:
+            pair_copy(i).wait()
+
+    def finish(step, carry):
+        rows = pl.ds(pl.multiple_of(step * TILE, TILE), TILE)
+        for at in range(width // (4 * BLOCK)):
+            columns = slice(at * 4 * BLOCK, (at + 1) * 4 * BLOCK)
+            total = own[rows, columns]
+            for turn in range(1, groups):
+                total = total + pair_in[turn - 1, rows, columns].astype(jnp.float32)
+            average = total * (1.0 / replicas)
+            moved = outer_mu * outer[rows, columns] + average
+            momentum[rows, columns] = moved
+            update[rows, columns] = (average + outer_mu * moved).astype(jnp.bfloat16)
+        return carry
+
+    lax.fori_loop(0, fragment // TILE, finish, 0)
+
+
+def exchange(codes, scales, outer_momentum, replicas):
+    fragment, width = outer_momentum.shape
+    groups = replicas // 2
+    dma = pltpu.SemaphoreType.DMA
+    vmem = pl.BlockSpec(memory_space=pltpu.VMEM)
+    return pl.pallas_call(
+        functools.partial(exchange_kernel, replicas),
+        out_shape=(
+            jax.ShapeDtypeStruct((fragment, width), jnp.float32),
+            jax.ShapeDtypeStruct((fragment, width), jnp.bfloat16),
+        ),
+        in_specs=[vmem] * 3,
+        out_specs=(vmem, vmem),
+        scratch_shapes=[
+            pltpu.VMEM((groups, fragment, width), jnp.bfloat16),
+            pltpu.VMEM((groups, fragment, BLOCK), jnp.bfloat16),
+            pltpu.VMEM((groups - 1, fragment, width), jnp.bfloat16),
+            pltpu.VMEM((groups - 1, fragment, width), jnp.bfloat16),
+            pltpu.VMEM((fragment, width), jnp.float32),
+            dma((groups * PARTS,)),
+            dma((groups * PARTS,)),
+            dma((groups,)),
+            dma((groups,)),
+            dma((groups * PARTS,)),
+            dma((groups * PARTS,)),
+        ],
+        compiler_params=pltpu.CompilerParams(
+            collective_id=0, has_side_effects=True, vmem_limit_bytes=40 * 2**20
+        ),
+    )(codes.reshape(replicas, fragment, width), scales.reshape(replicas, fragment, BLOCK), outer_momentum)
+
+
+def shards(weight, first_moment, second_moment, outer_momentum, act_table, token_ids, targets):
+    row_count, width = weight.shape
+    replicas = lax.axis_size("replica")
+    fragment = row_count // replicas
+    whole_tiles = fragment % TILE == 0 and width % (4 * BLOCK * PARTS) == 0 and width // BLOCK <= BLOCK
+    if not whole_tiles or replicas < 4 or replicas & (replicas - 1):
+        return shards_plain(
+            weight, first_moment, second_moment, outer_momentum, act_table, token_ids, targets
+        )
+    local = jnp.take(act_table, token_ids[0].reshape(-1), axis=0, mode="clip")
+    wanted = jnp.swapaxes(targets[0], 1, 2)
+    inputs = lax.all_gather(local, "mp", axis=1, tiled=True)
+    codes, scales = inner_steps(inputs, weight, first_moment[0], second_moment[0], wanted)
+    momentum, update = exchange(codes, scales, outer_momentum, replicas)
+    update = lax.all_gather(update, "replica", axis=0, tiled=True)
+    return (weight - outer_rate * update.astype(jnp.float32), momentum)
+
+
 def solution(mesh):
     in_specs = (
         P("mp", None),

time: 516 us -> 384 us (0.74); the launches traced: 508 us -> 384 us
  Pallas kernels: 0 us -> 169 us
  waiting for transfers between devices: 252 us -> 173 us
  matrix products: 73 us -> 0 us
  local copies, waits for them, and re-layouts: 76.3 us -> 15.3 us
  other arithmetic: 49.5 us -> 12.8 us
  blocking collectives: 31.3 us -> 0 us
  starting transfers between devices: 11.6 us -> 0.08 us
    pallas_call x0 -> x2, Pallas kernels: none -> 169 us  [the longest x1 89.9 us: exchange(): pl.pallas_call(functools.partial(exchange_kernel, replicas), out_shape=(j...]
    all_to_all x2 -> x0, waiting for transfers between devices: 122 us -> none  [the longest x1 122 us: shards(): lax.all_to_all(code_values.reshape(replicas, fragment, width), 'replica',...]
    dot_general x4 -> x0, matrix products: 73 us -> none  [the longest x2 41.4 us: shards(): lax.dot_general(signal, inputs, (((0,), (0,)), ((), ())), preferred_eleme...]
    all_gather x3 -> x2, waiting for transfers between devices: 130 us -> 173 us  [the longest x1 101 us: shards(): update = lax.all_gather(update, 'replica', axis=0, tiled=True)]
    all_gather x1 -> x0, blocking collectives: 31.3 us -> none  [shards(): lax.all_gather(update_scales, 'replica', axis=0, tiled=True)]
    mul x3 -> x0, local copies, waits for them, and re-layouts: 25.3 us -> none  [decode(): blocks * scales.astype(jnp.float32)[:, :, None]]
    div x3 -> x0, local copies, waits for them, and re-layouts: 22.1 us -> none  [encode(): blocks / scales.astype(jnp.float32)[:, :, None]]
    convert_element_type x4 -> x0, other arithmetic: 13.5 us -> none  [the longest x2 13.5 us: encode(): (blocks / scales.astype(jnp.float32)[:, :, None]).astype(jnp.bfloat16)]
  transfers between devices with their start and end apart: 5 -> 2, of which waited for: 4 -> 2; matrix products, arithmetic and copies ran while one was open for 12% -> 0% of each run, Pallas kernels for 0% -> 0%
where the time goes in v1:
time: 384 us
  waiting for transfers between devices  173 us (45%)
  Pallas kernels  169 us (44%)
  local copies, waits for them, and re-layouts  15.3 us (4%)
  between operations  14.1 us (4%)
  other arithmetic  12.8 us (3%)
    all_gather x1, waiting for transfers between devices, shards(): update = lax.all_gather(update, 'replica', axis=0, tiled=True)  101 us
    pallas_call x1, Pallas kernels, exchange(): pl.pallas_call(functools.partial(exchange_kernel, replicas), out_shape=(j...  89.9 us
    pallas_call x1, Pallas kernels, inner_steps(): pl.pallas_call(functools.partial(inner_kernel, chunks, factor, factor / t...  78.7 us
    all_gather x1, waiting for transfers between devices, shards(): inputs = lax.all_gather(local, 'mp', axis=1, tiled=True)  72.2 us
    sub x1, other arithmetic, shards(): return (weight - outer_rate * update.astype(jnp.float32), momentum)  12.8 us
    gather x1, local copies, waits for them, and re-layouts, shards(): local = jnp.take(act_table, token_ids[0].reshape(-1), axis=0, mode='clip')  9.85 us
  transfers between devices with their start and end apart: 2, of which 2 were waited for; matrix products, arithmetic and copies ran while one was open for 0% of the time, Pallas kernels for 0%

profile of v1, /device:TPU:0, one launch (start us, length us, event | category | flops | bytes accessed | tf_op | source)
XLA Modules:
  0.0 383.7 jit_solution(14827481146505725321)
XLA Ops:
  7.2 0.0 all-gather.6.cloned.1.call-start
  7.2 0.7 copy.10
  7.9 0.0 copy-start.2
  7.9 9.8 %gather_fusion = bf16[1024,1280]{1,0:T(8,128)(2,1)} fusion(bf16[2048,1280]{1,0:T(8,128)(2,1)} %param.11, s32[1024]{0:T(1024)S(1)} %broadcast_clamp_fusion), kind=kCustom, calls=%fused_computation | custom fusion | bytes 5246976 | tf_op jit(solution)/shard_map/jit(_take)/gather | solution.py:406
  17.8 0.0 all-gather.6.cloned.1.call-update
  17.8 0.0 all-gather.4.cloned.1.call-start
  17.8 0.0 copy-done.2
  17.8 0.7 copy.9
  18.5 0.1 slice_bitcast_fusion
  18.6 72.2 %all-gather.6.cloned.1.call-done.x1.x2 = bf16[1024,5120]{1,0:T(8,128)(2,1)} async-done(((bf16[1024,1280]{1,0:T(8,128)(2,1)}), bf16[1024,5120]{1,0:T(8,128)(2,1)}) %all-gather.6.cloned.1.call-update) | async-done | bytes 10485776 | tf_op jit(solution)/shard_map/all_gather | solution.py:408
  90.8 0.0 copy-start.1
  90.8 78.7 %shard_map.86 = (bf16[640,5120]{1,0:T(8,128)(2,1)}, bf16[640,128]{1,0:T(8,128)(2,1)S(1)}) custom-call(bf16[1024,5120]{1,0:T(8,128)(2,1)} %all-gather.6.cloned.1.call-done.x1.x2, bf16[1024,5120]{1,0:T(8,128)(2,1)} %all-gather.6.cloned.1.call-done.x1.x2, f32[640,5120]{1,0:T(8,128)} %w.1, bf16[640,5120]{1,0:T(8,128)(2,1)} %bitcast.18, ...), custom_call_target="tpu_custom_call" | custom-call | flops 13421772800 | bytes 98304000 | tf_op jit(solution)/shard_map/pallas_call | solution.py:210
  169.5 0.0 copy-done.1
  169.5 0.0 copy-start
  169.5 2.9 copy-done
  172.4 89.9 %shard_map.87 = (f32[80,5120]{1,0:T(8,128)S(1)}, bf16[80,5120]{1,0:T(8,128)(2,1)}) custom-call(bf16[8,80,5120]{2,1,0:T(8,128)(2,1)S(1)} %bitcast.13, bf16[8,80,128]{2,1,0:T(8,128)(2,1)S(1)} %bitcast.14, f32[80,5120]{1,0:T(8,128)S(1)} %copy-done.1), custom_call_target="tpu_custom_call" | custom-call | tf_op jit(solution)/shard_map/pallas_call | solution.py:370
  262.3 0.0 all-gather.4.cloned.1.call-update
  262.3 100.5 %all-gather.4.cloned.1.call-done = bf16[640,5120]{1,0:T(8,128)(2,1)} async-done(((bf16[80,5120]{1,0:T(8,128)(2,1)}), bf16[640,5120]{1,0:T(8,128)(2,1)}) %all-gather.4.cloned.1.call-update) | async-done | bytes 6553616 | tf_op jit(solution)/shard_map/all_gather | solution.py:411
  362.8 12.8 %multiply_subtract_fusion = f32[640,5120]{1,0:T(8,128)} fusion(f32[640,5120]{1,0:T(8,128)} %w.1, bf16[640,5120]{1,0:T(8,128)(2,1)} %all-gather.4.cloned.1.call-done), kind=kLoop, calls=%fused_computation.1 | loop fusion | flops 9830400 | bytes 32768000 | tf_op jit(solution)/shard_map/sub | solution.py:412
  375.7 1.2 copy.12
  (1 shorter events, 0.0 us)
Async XLA Ops:
  7.2 83.7 %all-gather.6.cloned.1.call-start = ((), (), s32[]{:S(2)}) async-start(), calls=%async_computation.1 | async-start | bytes 13107200 | tf_op jit(solution)/shard_map/all_gather | solution.py:408
  7.9 9.9 %copy-start.2 = (bf16[1,2,512,640]{3,2,1,0:T(8,128)(2,1)S(1)}, bf16[1,2,512,640]{3,2,1,0:T(8,128)(2,1)}, u32[]{:S(2)}) copy-start(bf16[1,2,512,640]{3,2,1,0:T(8,128)(2,1)} %param.13) | copy-start | bytes 3932164
  17.8 345.0 %all-gather.4.cloned.1.call-start = ((), (), s32[]{:S(2)}) async-start(), calls=%async_computation | async-start | bytes 7372800 | tf_op jit(solution)/shard_map/all_gather | solution.py:411
  90.8 78.7 %copy-start.1 = (f32[80,5120]{1,0:T(8,128)S(1)}, f32[80,5120]{1,0:T(8,128)}, u32[]{:S(2)}) copy-start(f32[80,5120]{1,0:T(8,128)} %outer.1) | copy-start | bytes 4915204
  169.5 2.9 copy-start
Sparse Core Ops, SparseCore 0:
  17.9 72.8 all-gather.5
  262.4 100.3 all-gather.3

commit v2 on v1

--- a/solution.py
+++ b/solution.py
@@ -113,63 +113,77 @@
     one = beta_first * moment_one + ((1.0 - beta_first) * unit) * gradient
     two = beta_second * moment_two + ((1.0 - beta_second) * unit * unit) * (gradient * gradient)
     spread = two * (1.0 / (1.0 - beta_second**step_count))
-    bottom = spread * lax.rsqrt(spread) + adam_epsilon
-    update = (one * (inner_rate / (1.0 - beta_first**step_count))) / bottom
+    root = lax.rsqrt(spread)
+    bottom = spread * root + adam_epsilon
+    inverse = root * (2.0 - bottom * root)
+    update = (one * (inner_rate / (1.0 - beta_first**step_count))) * inverse
     return (1.0 - inner_rate * weight_decay) * current - update, one, two
 
 
-def inner_kernel(
-    chunks, factor, unit, x1, x2, w, m, v, t1, t2, codes, scales, acc, s1, s2, g1, g2, half, all_scales
+def rows_of(i):
+    return pl.ds(pl.multiple_of(i * TILE, TILE), TILE)
+
+
+def add_output(chunk, chunks, factor, weights, inputs, wanted, acc, signal):
+    part = lax.dot_general(
+        weights, inputs, (((1,), (1,)), ((), ())), preferred_element_type=jnp.float32
+    )
+
+    @pl.when(chunk == 0)
+    def _():
+        acc[...] = part
+
+    @pl.when(chunk > 0)
+    def _():
+        acc[...] += part
+
+    @pl.when(chunk == chunks - 1)
+    def _():
+        signal[...] = (acc[...] * factor - wanted[...].astype(jnp.float32)).astype(jnp.bfloat16)
+
+
+def first_kernel(chunks, factor, unit, x, w, m, v, t, current, first, second, acc, signal, gradient):
+    phase, chunk = pl.program_id(0), pl.program_id(1)
+    row_count, wide = w.shape
+
+    @pl.when(phase == 0)
+    def _():
+        add_output(chunk, chunks, factor, w[...].astype(jnp.bfloat16), x[...], t, acc, signal)
+
+    @pl.when(phase == 1)
+    def _():
+        gradient[...] = jnp.dot(signal[...], x[...], preferred_element_type=jnp.float32)
+
+        def body(i, carry):
+            rows = rows_of(i)
+            for start in range(0, wide, 4 * BLOCK):
+                columns = slice(start, min(start + 4 * BLOCK, wide))
+                current[rows, columns], first[rows, columns], second[rows, columns] = adam(
+                    w[rows, columns],
+                    m[rows, columns].astype(jnp.float32),
+                    v[rows, columns].astype(jnp.float32),
+                    gradient[rows, columns],
+                    unit,
+                    PRIOR_STEPS + 1,
+                )
+            return carry
+
+        lax.fori_loop(0, row_count // TILE, body, 0)
+
+
+def second_kernel(
+    chunks, factor, unit, x, w, current, first, second, t, codes, scales, acc, signal, gradient, all_scales
 ):
     phase, chunk = pl.program_id(0), pl.program_id(1)
     row_count, wide = w.shape
-    rows_of = lambda i: pl.ds(pl.multiple_of(i * TILE, TILE), TILE)
-
-    def add_output(weights, inputs, wanted, signal):
-        part = lax.dot_general(
-            weights, inputs, (((1,), (1,)), ((), ())), preferred_element_type=jnp.float32
-        )
-
-        @pl.when(chunk == 0)
-        def _():
-            acc[...] = part
-
-        @pl.when(chunk > 0)
-        def _():
-            acc[...] += part
-
-        @pl.when(chunk == chunks - 1)
-        def _():
-            signal[...] = (acc[...] * factor - wanted[...].astype(jnp.float32)).astype(jnp.bfloat16)
-
-    def first_step(rows):
-        return adam(
-            w[rows, :],
-            m[rows, :].astype(jnp.float32),
-            v[rows, :].astype(jnp.float32),
-            g1[chunk, rows, :],
-            unit,
-            PRIOR_STEPS + 1,
-        )
 
     @pl.when(phase == 0)
     def _():
-        add_output(w[...].astype(jnp.bfloat16), x1[...], t1, s1)
+        add_output(chunk, chunks, factor, current[...].astype(jnp.bfloat16), x[...], t, acc, signal)
 
     @pl.when(phase == 1)
     def _():
-        g1[chunk] = jnp.dot(s1[...], x1[...], preferred_element_type=jnp.float32)
-
-        def body(i, carry):
-            half[rows_of(i), :] = first_step(rows_of(i))[0].astype(jnp.bfloat16)
-            return carry
-
-        lax.fori_loop(0, row_count // TILE, body, 0, unroll=2)
-        add_output(half[...], x2[...], t2, s2)
-
-    @pl.when(phase == 2)
-    def _():
-        g2[...] = jnp.dot(s2[...], x2[...], preferred_element_type=jnp.float32)
+        gradient[...] = jnp.dot(signal[...], x[...], preferred_element_type=jnp.float32)
         lane = lax.broadcasted_iota(jnp.int32, (TILE, BLOCK), 1)
 
         @pl.when(chunk == 0)
@@ -178,69 +192,104 @@
 
         def body(i, carry):
             rows = rows_of(i)
-            current, one, two = first_step(rows)
-            current, _, _ = adam(current, one, two, g2[rows, :], unit, PRIOR_STEPS + 2)
-            delta = w[rows, :] - current
             kept = all_scales[rows, :]
             for block in range(wide // BLOCK):
-                values = delta[:, block * BLOCK : (block + 1) * BLOCK]
+                columns = slice(block * BLOCK, (block + 1) * BLOCK)
+                after, _, _ = adam(
+                    current[rows, columns],
+                    first[rows, columns],
+                    second[rows, columns],
+                    gradient[rows, columns],
+                    unit,
+                    PRIOR_STEPS + 2,
+                )
+                values = w[rows, columns] - after
                 largest = jnp.max(jnp.abs(values), axis=1, keepdims=True)
                 scale = (largest + scale_epsilon).astype(jnp.bfloat16).astype(jnp.float32)
-                codes[rows, block * BLOCK : (block + 1) * BLOCK] = (values / scale).astype(jnp.bfloat16)
+                codes[rows, columns] = (values / scale).astype(jnp.bfloat16)
                 kept = jnp.where(lane == chunk * (wide // BLOCK) + block, scale, kept)
             all_scales[rows, :] = kept
             return carry
 
-        lax.fori_loop(0, row_count // TILE, body, 0, unroll=2)
+        lax.fori_loop(0, row_count // TILE, body, 0)
 
         @pl.when(chunk == chunks - 1)
         def _():
             scales[...] = all_scales[...].astype(jnp.bfloat16)
 
 
-def inner_steps(inputs, weight, first, second, wanted):
+def first_step(inputs, weight, first, second, wanted):
     row_count, width = weight.shape
-    tokens = wanted.shape[2]
-    wide = 512 if width % 512 == 0 else BLOCK
+    tokens = inputs.shape[0]
+    wide = next(size for size in (1024, 512, BLOCK) if width % size == 0)
     chunks = width // wide
     factor = width ** (-0.5)
-    later = lambda phase, chunk: chunk * jnp.minimum(phase, 1)
     columns = lambda phase, chunk: (0, chunk)
+    later = lambda phase, chunk: (0, chunk * phase)
+    kept = jax.ShapeDtypeStruct((row_count, width), jnp.float32)
+    return pl.pallas_call(
+        functools.partial(first_kernel, chunks, factor, factor / tokens),
+        grid=(2, chunks),
+        out_shape=(kept, kept, kept),
+        in_specs=[
+            pl.BlockSpec((tokens, wide), columns),
+            pl.BlockSpec((row_count, wide), columns),
+            pl.BlockSpec((row_count, wide), later),
+            pl.BlockSpec((row_count, wide), later),
+            pl.BlockSpec((row_count, tokens), lambda phase, chunk: (0, 0)),
+        ],
+        out_specs=(pl.BlockSpec((row_count, wide), later),) * 3,
+        scratch_shapes=[
+            pltpu.VMEM((row_count, tokens), jnp.float32),
+            pltpu.VMEM((row_count, tokens), jnp.bfloat16),
+            pltpu.VMEM((row_count, wide), jnp.float32),
+        ],
+        compiler_params=pltpu.CompilerParams(vmem_limit_bytes=48 * 2**20),
+        cost_estimate=pl.CostEstimate(
+            flops=4 * row_count * width * tokens, bytes_accessed=24 * row_count * width, transcendentals=0
+        ),
+    )(inputs, weight, first, second, wanted)
+
+
+def second_step(inputs, weight, current, first, second, wanted):
+    row_count, width = weight.shape
+    tokens = inputs.shape[0]
+    wide = next(size for size in (1024, 512, BLOCK) if width % size == 0)
+    chunks = width // wide
+    factor = width ** (-0.5)
+    columns = lambda phase, chunk: (0, chunk)
+    later = lambda phase, chunk: (0, chunk * phase)
     whole = lambda phase, chunk: (0, 0)
     return pl.pallas_call(
-        functools.partial(inner_kernel, chunks, factor, factor / tokens),
-        grid=(3, chunks),
+        functools.partial(second_kernel, chunks, factor, factor / tokens),
+        grid=(2, chunks),
         out_shape=(
             jax.ShapeDtypeStruct((row_count, width), jnp.bfloat16),
             jax.ShapeDtypeStruct((row_count, BLOCK), jnp.bfloat16),
         ),
         in_specs=[
-            pl.BlockSpec((tokens, wide), lambda phase, chunk: (0, jnp.where(phase < 2, chunk, chunks - 1))),
-            pl.BlockSpec((tokens, wide), lambda phase, chunk: (1, later(phase, chunk))),
+            pl.BlockSpec((tokens, wide), columns),
+            pl.BlockSpec((row_count, wide), later),
             pl.BlockSpec((row_count, wide), columns),
-            pl.BlockSpec((row_count, wide), lambda phase, chunk: (0, later(phase, chunk))),
-            pl.BlockSpec((row_count, wide), lambda phase, chunk: (0, later(phase, chunk))),
-            pl.BlockSpec((row_count, tokens), whole),
+            pl.BlockSpec((row_count, wide), later),
+            pl.BlockSpec((row_count, wide), later),
             pl.BlockSpec((row_count, tokens), whole),
         ],
         out_specs=(
-            pl.BlockSpec((row_count, wide), lambda phase, chunk: (0, chunk * (phase // 2))),
+            pl.BlockSpec((row_count, wide), later),
             pl.BlockSpec((row_count, BLOCK), whole),
         ),
         scratch_shapes=[
             pltpu.VMEM((row_count, tokens), jnp.float32),
             pltpu.VMEM((row_count, tokens), jnp.bfloat16),
-            pltpu.VMEM((row_count, tokens), jnp.bfloat16),
-            pltpu.VMEM((chunks, row_count, wide), jnp.float32),
             pltpu.VMEM((row_count, wide), jnp.float32),
-            pltpu.VMEM((row_count, wide), jnp.bfloat16),
             pltpu.VMEM((row_count, BLOCK), jnp.float32),
         ],
         compiler_params=pltpu.CompilerParams(vmem_limit_bytes=48 * 2**20),
         cost_estimate=pl.CostEstimate(
-            flops=8 * row_count * width * tokens, bytes_accessed=30 * row_count * width, transcendentals=0
-        ),
-    )(inputs, inputs, weight, first, second, wanted[0], wanted[1])
+            flops=4 * row_count * width * tokens, bytes_accessed=22 * row_count * width, transcendentals=0
+        ),
+    )(inputs, weight, current, first, second, wanted)
 
 
 def flipped(place, bits):
@@ -252,12 +301,14 @@
     return place
 
 
-PARTS = 2
+PARTS = 4
+AHEAD = 3
 
 
 def exchange_kernel(
-    replicas, codes, scales, outer, momentum, update, got_codes, got_scales, pair_out, pair_in, own,
+    replicas, codes, scales, outer, momentum, updates, got_codes, got_scales, pair_out, pair_in, own, update,
     code_send, code_recv, scale_send, scale_recv, pair_send, pair_recv,
+    along_send, along_recv, across_send, across_recv, keep,
 ):
     groups = replicas // 2
     me = lax.axis_index("replica")
@@ -312,14 +363,14 @@
 
     for turn in range(groups):
         scale_copy(turn).start()
-    code_copy(0).start()
-    code_copy(1).start()
+    for i in range(AHEAD):
+        code_copy(i).start()
     for i, (turn, part) in enumerate(order):
         if part == 0:
             scale_copy(turn).wait()
         code_copy(i).wait()
-        if i + 2 < len(order):
-            code_copy(i + 2).start()
+        if i + AHEAD < len(order):
+            code_copy(i + AHEAD).start()
         mine = 2 * flipped(group, turn) + side
 
         def body(step, carry):
@@ -342,24 +393,77 @@
         lax.fori_loop(0, fragment // TILE, body, 0)
         if turn:
             pair_copy(i).start()
-    for i, (turn, part) in enumerate(order):
-        if turn:
-            pair_copy(i).wait()
-
-    def finish(step, carry):
-        rows = pl.ds(pl.multiple_of(step * TILE, TILE), TILE)
-        for at in range(width // (4 * BLOCK)):
-            columns = slice(at * 4 * BLOCK, (at + 1) * 4 * BLOCK)
-            total = own[rows, columns]
-            for turn in range(1, groups):
-                total = total + pair_in[turn - 1, rows, columns].astype(jnp.float32)
-            average = total * (1.0 / replicas)
-            moved = outer_mu * outer[rows, columns] + average
-            momentum[rows, columns] = moved
-            update[rows, columns] = (average + outer_mu * moved).astype(jnp.bfloat16)
-        return carry
-
-    lax.fori_loop(0, fragment // TILE, finish, 0)
+    hops = []
+    bit = groups // 2
+    while bit:
+        hops += [(bit, held) for held in range(0, groups, 2 * bit)]
+        bit //= 2
+
+    def place_of(held, part):
+        return updates.at[2 * flipped(group, held) + side, :, pl.ds(part * wide, wide)]
+
+    def source_of(held, part):
+        return update.at[:, pl.ds(part * wide, wide)] if held == 0 else place_of(held, part)
+
+    def along_copy(hop, part):
+        bit, held = hops[hop]
+        return pltpu.make_async_remote_copy(
+            src_ref=source_of(held, part),
+            dst_ref=place_of(held, part),
+            send_sem=along_send.at[hop * PARTS + part],
+            recv_sem=along_recv.at[hop * PARTS + part],
+            device_id={"replica": 2 * flipped(group, bit) + side},
+            device_id_type=MESH,
+        )
+
+    def across_copy(held, part):
+        return pltpu.make_async_remote_copy(
+            src_ref=source_of(held, part),
+            dst_ref=place_of(held, part),
+            send_sem=across_send.at[held * PARTS + part],
+            recv_sem=across_recv.at[held * PARTS + part],
+            device_id={"replica": partner},
+            device_id_type=MESH,
+        )
+
+    def send_on(held, part):
+        for hop, (bit, taken) in enumerate(hops):
+            if taken == held:
+                along_copy(hop, part).start()
+        across_copy(held, part).start()
+
+    for part in range(PARTS):
+        for i, (turn, which) in enumerate(order):
+            if turn and which == part:
+                pair_copy(i).wait()
+
+        def finish(step, carry):
+            rows = pl.ds(pl.multiple_of(step * TILE, TILE), TILE)
+            for start in range(part * wide, (part + 1) * wide, 2 * BLOCK):
+                columns = slice(start, start + 2 * BLOCK)
+                total = own[rows, columns]
+                for turn in range(1, groups):
+                    total = total + pair_in[turn - 1, rows, columns].astype(jnp.float32)
+                average = total * (1.0 / replicas)
+                moved = outer_mu * outer[rows, columns] + average
+                momentum[rows, columns] = moved
+                update[rows, columns] = (average + outer_mu * moved).astype(jnp.bfloat16)
+            return carry
+
+        lax.fori_loop(0, fragment // TILE, finish, 0)
+        send_on(0, part)
+    own_copy = pltpu.make_async_copy(update, updates.at[me], keep)
+    own_copy.start()
+    for hop, (bit, held) in enumerate(hops):
+        for part in range(PARTS):
+            along_copy(hop, part).wait_recv()
+            send_on(held + bit, part)
+    own_copy.wait()
+    for part in range(PARTS):
+        for hop in range(len(hops)):
+            along_copy(hop, part).wait_send()
+        for held in range(groups):
+            across_copy(held, part).wait()
 
 
 def exchange(codes, scales, outer_momentum, replicas):
@@ -371,22 +475,28 @@
         functools.partial(exchange_kernel, replicas),
         out_shape=(
             jax.ShapeDtypeStruct((fragment, width), jnp.float32),
-            jax.ShapeDtypeStruct((fragment, width), jnp.bfloat16),
+            jax.ShapeDtypeStruct((replicas, fragment, width), jnp.bfloat16),
         ),
         in_specs=[vmem] * 3,
-        out_specs=(vmem, vmem),
+        out_specs=(vmem, pl.BlockSpec(memory_space=pl.ANY)),
         scratch_shapes=[
             pltpu.VMEM((groups, fragment, width), jnp.bfloat16),
             pltpu.VMEM((groups, fragment, BLOCK), jnp.bfloat16),
             pltpu.VMEM((groups - 1, fragment, width), jnp.bfloat16),
             pltpu.VMEM((groups - 1, fragment, width), jnp.bfloat16),
             pltpu.VMEM((fragment, width), jnp.float32),
+            pltpu.VMEM((fragment, width), jnp.bfloat16),
             dma((groups * PARTS,)),
             dma((groups * PARTS,)),
             dma((groups,)),
             dma((groups,)),
             dma((groups * PARTS,)),
             dma((groups * PARTS,)),
+            dma(((groups - 1) * PARTS,)),
+            dma(((groups - 1) * PARTS,)),
+            dma((groups * PARTS,)),
+            dma((groups * PARTS,)),
+            dma,
         ],
         compiler_params=pltpu.CompilerParams(
             collective_id=0, has_side_effects=True, vmem_limit_bytes=40 * 2**20
@@ -398,18 +508,23 @@
     row_count, width = weight.shape
     replicas = lax.axis_size("replica")
     fragment = row_count // replicas
-    whole_tiles = fragment % TILE == 0 and width % (4 * BLOCK * PARTS) == 0 and width // BLOCK <= BLOCK
+    whole_tiles = fragment % TILE == 0 and width % (2 * BLOCK * PARTS) == 0 and width // BLOCK <= BLOCK
     if not whole_tiles or replicas < 4 or replicas & (replicas - 1):
         return shards_plain(
             weight, first_moment, second_moment, outer_momentum, act_table, token_ids, targets
         )
-    local = jnp.take(act_table, token_ids[0].reshape(-1), axis=0, mode="clip")
     wanted = jnp.swapaxes(targets[0], 1, 2)
-    inputs = lax.all_gather(local, "mp", axis=1, tiled=True)
-    codes, scales = inner_steps(inputs, weight, first_moment[0], second_moment[0], wanted)
-    momentum, update = exchange(codes, scales, outer_momentum, replicas)
-    update = lax.all_gather(update, "replica", axis=0, tiled=True)
-    return (weight - outer_rate * update.astype(jnp.float32), momentum)
+    inputs = [
+        lax.all_gather(
+            jnp.take(act_table, token_ids[0, step], axis=0, mode="clip"), "mp", axis=1, tiled=True
+        )
+        for step in range(STEPS)
+    ]
+    current, first, second = first_step(inputs[0], weight, first_moment[0], second_moment[0], wanted[0])
+    codes, scales = second_step(inputs[1], weight, current, first, second, wanted[1])
+    momentum, updates = exchange(codes, scales, outer_momentum, replicas)
+    update = updates.reshape(row_count, width).astype(jnp.float32)
+    return (weight - outer_rate * update, momentum)
 
 
 def solution(mesh):

time: 384 us -> 341 us (0.89)
  waiting for transfers between devices: 173 us -> 39.6 us
  Pallas kernels: 169 us -> 244 us
  other arithmetic: 12.8 us -> 21 us
  local copies, waits for them, and re-layouts: 15.3 us -> 21.9 us
    all_gather x2, waiting for transfers between devices: 173 us -> 39.5 us  [shards(): lax.all_gather(jnp.take(act_table, token_ids[0, step], axis=0, mode='clip...]
    pallas_call x1, Pallas kernels: 89.9 us -> 163 us  [exchange(): pl.pallas_call(functools.partial(exchange_kernel, replicas), out_shape=(j...]
    mul x0 -> x1, other arithmetic: none -> 6.49 us  [shards(): return (weight - outer_rate * update, momentum)]
    gather x1 -> x2, local copies, waits for them, and re-layouts: 9.85 us -> 14.2 us  [shards(): jnp.take(act_table, token_ids[0, step], axis=0, mode='clip')]
    pallas_call x1 -> x2, Pallas kernels: 78.7 us -> 80.8 us  [the longest x1 45.1 us: second_step(): pl.pallas_call(functools.partial(second_kernel, chunks, factor, factor /...]
  transfers between devices with their start and end apart: 2 -> 2, of which waited for: 2 -> 2; matrix products, arithmetic and copies ran while one was open for 0% -> 2% of each run, Pallas kernels for 0% -> 10%
where the time goes in v2:
time: 341 us
  Pallas kernels  244 us (72%)
  waiting for transfers between devices  39.6 us (12%)
  local copies, waits for them, and re-layouts  21.9 us (6%)
  other arithmetic  21 us (6%)
  between operations  14.1 us (4%)
    pallas_call x1, Pallas kernels, exchange(): pl.pallas_call(functools.partial(exchange_kernel, replicas), out_shape=(j...  163 us
    pallas_call x1, Pallas kernels, second_step(): pl.pallas_call(functools.partial(second_kernel, chunks, factor, factor /...  45.1 us
    all_gather x2, waiting for transfers between devices, shards(): lax.all_gather(jnp.take(act_table, token_ids[0, step], axis=0, mode='clip...  39.5 us
    pallas_call x1, Pallas kernels, first_step(): pl.pallas_call(functools.partial(first_kernel, chunks, factor, factor / t...  35.7 us
    sub x1, other arithmetic, shards(): return (weight - outer_rate * update, momentum)  14.5 us
    gather x2, local copies, waits for them, and re-layouts, shards(): jnp.take(act_table, token_ids[0, step], axis=0, mode='clip')  14.2 us
  transfers between devices with their start and end apart: 2, of which 2 were waited for; matrix products, arithmetic and copies ran while one was open for 2% of the time, Pallas kernels for 10%

profile of v2, /device:TPU:0, one launch (start us, length us, event | category | flops | bytes accessed | tf_op | source)
XLA Modules:
  0.0 340.8 jit_solution(10511206597047885838)
XLA Ops:
  7.2 0.0 all-gather.7.cloned.1.call-start
  7.2 0.8 fusion
  8.0 7.1 %gather_fusion.1 = bf16[512,1280]{1,0:T(8,128)(2,1)} fusion(bf16[2048,1280]{1,0:T(8,128)(2,1)} %param.11, s32[1024]{0:T(1024)S(1)} %pad_clamp_fusion), kind=kCustom, calls=%fused_computation.1 | custom fusion | bytes 2623488 | tf_op jit(solution)/shard_map/jit(_take)/gather | solution.py:519
  15.1 0.0 all-gather.7.cloned.1.call-update
  15.1 0.2 all-gather.5.cloned.1.call-start
  15.3 0.0 copy-start.3
  15.3 7.2 %gather_fusion = bf16[512,1280]{1,0:T(8,128)(2,1)} fusion(bf16[2048,1280]{1,0:T(8,128)(2,1)} %param.11, s32[1024]{0:T(1024)S(1)} %pad_clamp_fusion.1), kind=kCustom, calls=%fused_computation | custom fusion | bytes 2623488 | tf_op jit(solution)/shard_map/jit(_take)/gather | solution.py:519
  22.5 0.0 all-gather.5.cloned.1.call-update
  22.5 0.0 copy-done.3
  22.5 0.7 copy.9
  23.2 0.1 slice_bitcast_fusion
  23.3 35.1 %all-gather.7.cloned.1.call-done.x = bf16[512,5120]{1,0:T(8,128)(2,1)} async-done(((bf16[512,1280]{1,0:T(8,128)(2,1)}), bf16[512,5120]{1,0:T(8,128)(2,1)}) %all-gather.7.cloned.1.call-update) | async-done | bytes 5242896 | tf_op jit(solution)/shard_map/all_gather | solution.py:518
  58.4 0.0 copy-start.1
  58.4 2.5 copy-done.1
  60.9 35.7 %shard_map.86 = (f32[640,5120]{1,0:T(8,128)}, f32[640,5120]{1,0:T(8,128)}, f32[640,5120]{1,0:T(8,128)}) custom-call(bf16[512,5120]{1,0:T(8,128)(2,1)S(1)} %copy-done.1, f32[640,5120]{1,0:T(8,128)} %w.3, bf16[640,5120]{1,0:T(8,128)(2,1)} %bitcast.17, bf16[640,5120]{1,0:T(8,128)(2,1)} %bitcast.18, bf16[640,512]{1,0:T(8,128)(2,1)S(1)} %get-tuple-element.17.t), custom_call_target="tpu_custom_call" | custom-call | flops 6710886400 | bytes 78643200 | tf_op jit(solution)/shard_map/pallas_call | solution.py:230
  96.5 4.5 %all-gather.5.cloned.1.call-done.x = bf16[512,5120]{1,0:T(8,128)(2,1)} async-done(((bf16[512,1280]{1,0:T(8,128)(2,1)}), bf16[512,5120]{1,0:T(8,128)(2,1)}) %all-gather.5.cloned.1.call-update) | async-done | bytes 5242896 | tf_op jit(solution)/shard_map/all_gather | solution.py:518
  101.0 0.0 copy-start
  101.0 2.5 copy-done
  103.5 0.0 copy-start.2
  103.5 45.1 %shard_map.87 = (bf16[640,5120]{1,0:T(8,128)(2,1)}, bf16[640,128]{1,0:T(8,128)(2,1)S(1)}) custom-call(bf16[512,5120]{1,0:T(8,128)(2,1)S(1)} %copy-done, f32[640,5120]{1,0:T(8,128)} %w.3, f32[640,5120]{1,0:T(8,128)} %get-tuple-element.9.current, f32[640,5120]{1,0:T(8,128)} %get-tuple-element.10.first, f32[640,5120]{1,0:T(8,128)} %get-tuple-element.11.second, ...), custom_call_target="tpu_custom_call" | custom-call | flops 6710886400 | bytes 72089600 | tf_op jit(solution)/shard_map/pallas_call | solution.py:263
  148.6 0.0 copy-done.2
  148.6 163.2 %shard_map.88 = (f32[80,5120]{1,0:T(8,128)S(1)}, bf16[8,80,5120]{2,1,0:T(8,128)(2,1)S(1)}) custom-call(bf16[8,80,5120]{2,1,0:T(8,128)(2,1)} %bitcast.16, bf16[8,80,128]{2,1,0:T(8,128)(2,1)S(1)} %bitcast.15, f32[80,5120]{1,0:T(8,128)S(1)} %copy-done.2), custom_call_target="tpu_custom_call" | custom-call | tf_op jit(solution)/shard_map/pallas_call | solution.py:474
  311.7 6.5 %convert_multiply_fusion = f32[8,80,5120]{2,1,0:T(8,128)} fusion(bf16[8,80,5120]{2,1,0:T(8,128)(2,1)S(1)} %get-tuple-element.14), kind=kLoop, calls=%fused_computation.3 | loop fusion | flops 6553600 | bytes 19660800 | tf_op jit(solution)/shard_map/mul | solution.py:527
  318.2 14.5 %bitcast_subtract_fusion = f32[640,5120]{1,0:T(8,128)} fusion(f32[640,5120]{1,0:T(8,128)} %w.3, f32[8,80,5120]{2,1,0:T(8,128)} %convert_multiply_fusion), kind=kLoop, calls=%fused_computation.2 | loop fusion | flops 3276800 | bytes 39321600 | tf_op jit(solution)/shard_map/sub | solution.py:527
  332.8 1.2 copy.11
  (2 shorter events, 0.0 us)
Async XLA Ops:
  7.2 51.2 %all-gather.7.cloned.1.call-start = ((), (), s32[]{:S(2)}) async-start(), calls=%async_computation.1 | async-start | bytes 6553600 | tf_op jit(solution)/shard_map/all_gather | solution.py:518
  15.1 85.9 %all-gather.5.cloned.1.call-start = ((), (), s32[]{:S(2)}) async-start(), calls=%async_computation | async-start | bytes 6553600 | tf_op jit(solution)/shard_map/all_gather | solution.py:518
  15.3 7.2 %copy-start.3 = (bf16[1,2,512,640]{3,2,1,0:T(8,128)(2,1)S(1)}, bf16[1,2,512,640]{3,2,1,0:T(8,128)(2,1)}, u32[]{:S(2)}) copy-start(bf16[1,2,512,640]{3,2,1,0:T(8,128)(2,1)} %param.13) | copy-start | bytes 3932164
  58.4 2.5 copy-start.1
  101.0 2.5 copy-start
  103.5 45.1 %copy-start.2 = (f32[80,5120]{1,0:T(8,128)S(1)}, f32[80,5120]{1,0:T(8,128)}, u32[]{:S(2)}) copy-start(f32[80,5120]{1,0:T(8,128)} %outer.1) | copy-start | bytes 4915204
Sparse Core Ops, SparseCore 0:
  15.2 43.1 all-gather.6
  60.5 40.4 all-gather.4

commit v3 on v2

--- a/solution.py
+++ b/solution.py
@@ -142,17 +142,27 @@
         signal[...] = (acc[...] * factor - wanted[...].astype(jnp.float32)).astype(jnp.bfloat16)
 
 
-def first_kernel(chunks, factor, unit, x, w, m, v, t, current, first, second, acc, signal, gradient):
+def keep_piece(chunk, pieces, kept):
+    for place, piece in enumerate(pieces):
+
+        @pl.when(chunk == place)
+        def _():
+            kept[place] = piece[...]
+
+
+def first_kernel(chunks, factor, unit, places, *refs):
+    pieces, (w, m, v, t, current, first, second, acc, signal, gradient, x) = refs[:chunks], refs[chunks:]
     phase, chunk = pl.program_id(0), pl.program_id(1)
     row_count, wide = w.shape
 
     @pl.when(phase == 0)
     def _():
-        add_output(chunk, chunks, factor, w[...].astype(jnp.bfloat16), x[...], t, acc, signal)
+        keep_piece(chunk, pieces, x)
+        add_output(chunk, chunks, factor, w[...].astype(jnp.bfloat16), x[chunk], t, acc, signal)
 
     @pl.when(phase == 1)
     def _():
-        gradient[...] = jnp.dot(signal[...], x[...], preferred_element_type=jnp.float32)
+        gradient[...] = jnp.dot(signal[...], x[chunk], preferred_element_type=jnp.float32)
 
         def body(i, carry):
             rows = rows_of(i)
@@ -171,19 +181,20 @@
         lax.fori_loop(0, row_count // TILE, body, 0)
 
 
-def second_kernel(
-    chunks, factor, unit, x, w, current, first, second, t, codes, scales, acc, signal, gradient, all_scales
-):
+def second_kernel(chunks, factor, unit, places, *refs):
+    pieces, refs = refs[:chunks], refs[chunks:]
+    w, current, first, second, t, codes, scales, acc, signal, gradient, all_scales, x = refs
     phase, chunk = pl.program_id(0), pl.program_id(1)
     row_count, wide = w.shape
 
     @pl.when(phase == 0)
     def _():
-        add_output(chunk, chunks, factor, current[...].astype(jnp.bfloat16), x[...], t, acc, signal)
+        keep_piece(chunk, pieces, x)
+        add_output(chunk, chunks, factor, current[...].astype(jnp.bfloat16), x[chunk], t, acc, signal)
 
     @pl.when(phase == 1)
     def _():
-        gradient[...] = jnp.dot(signal[...], x[...], preferred_element_type=jnp.float32)
+        gradient[...] = jnp.dot(signal[...], x[chunk], preferred_element_type=jnp.float32)
         lane = lax.broadcasted_iota(jnp.int32, (TILE, BLOCK), 1)
 
         @pl.when(chunk == 0)
@@ -207,7 +218,7 @@
                 largest = jnp.max(jnp.abs(values), axis=1, keepdims=True)
                 scale = (largest + scale_epsilon).astype(jnp.bfloat16).astype(jnp.float32)
                 codes[rows, columns] = (values / scale).astype(jnp.bfloat16)
-                kept = jnp.where(lane == chunk * (wide // BLOCK) + block, scale, kept)
+                kept = jnp.where(lane == places[chunk] * (wide // BLOCK) + block, scale, kept)
             all_scales[rows, :] = kept
             return carry
 
@@ -218,62 +229,69 @@
             scales[...] = all_scales[...].astype(jnp.bfloat16)
 
 
-def first_step(inputs, weight, first, second, wanted):
+def first_step(places, pieces, weight, first, second, wanted):
     row_count, width = weight.shape
-    tokens = inputs.shape[0]
-    wide = next(size for size in (1024, 512, BLOCK) if width % size == 0)
-    chunks = width // wide
+    tokens, wide = pieces[0].shape
+    chunks = len(pieces)
     factor = width ** (-0.5)
-    columns = lambda phase, chunk: (0, chunk)
-    later = lambda phase, chunk: (0, chunk * phase)
+    columns = lambda phase, chunk, places: (0, places[chunk])
+    later = lambda phase, chunk, places: (0, places[chunk * phase])
     kept = jax.ShapeDtypeStruct((row_count, width), jnp.float32)
+    whole = lambda phase, chunk, places: (0, 0)
+    once = pl.Buffered(1)
     return pl.pallas_call(
         functools.partial(first_kernel, chunks, factor, factor / tokens),
-        grid=(2, chunks),
         out_shape=(kept, kept, kept),
-        in_specs=[
-            pl.BlockSpec((tokens, wide), columns),
+        grid_spec=pltpu.PrefetchScalarGridSpec(
+            num_scalar_prefetch=1,
+            grid=(2, chunks),
+        in_specs=[pl.BlockSpec((tokens, wide), whole, pipeline_mode=once)] * chunks
+        + [
             pl.BlockSpec((row_count, wide), columns),
             pl.BlockSpec((row_count, wide), later),
             pl.BlockSpec((row_count, wide), later),
-            pl.BlockSpec((row_count, tokens), lambda phase, chunk: (0, 0)),
+            pl.BlockSpec((row_count, tokens), whole, pipeline_mode=once),
         ],
         out_specs=(pl.BlockSpec((row_count, wide), later),) * 3,
         scratch_shapes=[
             pltpu.VMEM((row_count, tokens), jnp.float32),
             pltpu.VMEM((row_count, tokens), jnp.bfloat16),
             pltpu.VMEM((row_count, wide), jnp.float32),
+            pltpu.VMEM((chunks, tokens, wide), jnp.bfloat16),
         ],
-        compiler_params=pltpu.CompilerParams(vmem_limit_bytes=48 * 2**20),
+        ),
+        compiler_params=pltpu.CompilerParams(vmem_limit_bytes=56 * 2**20),
         cost_estimate=pl.CostEstimate(
             flops=4 * row_count * width * tokens, bytes_accessed=24 * row_count * width, transcendentals=0
         ),
-    )(inputs, weight, first, second, wanted)
-
-
-def second_step(inputs, weight, current, first, second, wanted):
+    )(places, *pieces, weight, first, second, wanted)
+
+
+def second_step(places, pieces, weight, current, first, second, wanted):
     row_count, width = weight.shape
-    tokens = inputs.shape[0]
-    wide = next(size for size in (1024, 512, BLOCK) if width % size == 0)
-    chunks = width // wide
+    tokens, wide = pieces[0].shape
+    chunks = len(pieces)
     factor = width ** (-0.5)
-    columns = lambda phase, chunk: (0, chunk)
-    later = lambda phase, chunk: (0, chunk * phase)
-    whole = lambda phase, chunk: (0, 0)
+    columns = lambda phase, chunk, places: (0, places[chunk])
+    later = lambda phase, chunk, places: (0, places[chunk * phase])
+    whole = lambda phase, chunk, places: (0, 0)
+    once = pl.Buffered(1)
     return pl.pallas_call(
         functools.partial(second_kernel, chunks, factor, factor / tokens),
-        grid=(2, chunks),
         out_shape=(
             jax.ShapeDtypeStruct((row_count, width), jnp.bfloat16),
             jax.ShapeDtypeStruct((row_count, BLOCK), jnp.bfloat16),
         ),
-        in_specs=[
-            pl.BlockSpec((tokens, wide), columns),
+        grid_spec=pltpu.PrefetchScalarGridSpec(
+            num_scalar_prefetch=1,
+            grid=(2, chunks),
+        in_specs=[pl.BlockSpec((tokens, wide), whole, pipeline_mode=once)] * chunks
+        + [
             pl.BlockSpec((row_count, wide), later),
             pl.BlockSpec((row_count, wide), columns),
             pl.BlockSpec((row_count, wide), later),
             pl.BlockSpec((row_count, wide), later),
-            pl.BlockSpec((row_count, tokens), whole),
+            pl.BlockSpec((row_count, tokens), whole, pipeline_mode=once),
         ],
         out_specs=(
             pl.BlockSpec((row_count, wide), later),
@@ -284,12 +302,14 @@
             pltpu.VMEM((row_count, tokens), jnp.bfloat16),
             pltpu.VMEM((row_count, wide), jnp.float32),
             pltpu.VMEM((row_count, BLOCK), jnp.float32),
+            pltpu.VMEM((chunks, tokens, wide), jnp.bfloat16),
         ],
-        compiler_params=pltpu.CompilerParams(vmem_limit_bytes=48 * 2**20),
+        ),
+        compiler_params=pltpu.CompilerParams(vmem_limit_bytes=56 * 2**20),
         cost_estimate=pl.CostEstimate(
             flops=4 * row_count * width * tokens, bytes_accessed=22 * row_count * width, transcendentals=0
         ),
-    )(inputs, weight, current, first, second, wanted)
+    )(places, *pieces, weight, current, first, second, wanted)
 
 
 def flipped(place, bits):
@@ -302,7 +322,7 @@
 
 
 PARTS = 4
-AHEAD = 3
+AHEAD = 4
 
 
 def exchange_kernel(
@@ -325,7 +345,7 @@
         )
     pl.semaphore_wait(barrier, groups)
 
-    order = [(turn, part) for turn in range(groups - 1, -1, -1) for part in range(PARTS)]
+    order = [(turn, part) for part in range(PARTS) for turn in range(groups - 1, -1, -1)]
 
     def code_copy(i):
         turn, part = order[i]
@@ -365,7 +385,8 @@
         scale_copy(turn).start()
     for i in range(AHEAD):
         code_copy(i).start()
-    for i, (turn, part) in enumerate(order):
+    def add_pair(i):
+        turn, part = order[i]
         if part == 0:
             scale_copy(turn).wait()
         code_copy(i).wait()
@@ -393,6 +414,7 @@
         lax.fori_loop(0, fragment // TILE, body, 0)
         if turn:
             pair_copy(i).start()
+
     hops = []
     bit = groups // 2
     while bit:
@@ -432,7 +454,7 @@
                 along_copy(hop, part).start()
         across_copy(held, part).start()
 
-    for part in range(PARTS):
+    def finish_part(part):
         for i, (turn, which) in enumerate(order):
             if turn and which == part:
                 pair_copy(i).wait()
@@ -452,12 +474,22 @@
 
         lax.fori_loop(0, fragment // TILE, finish, 0)
         send_on(0, part)
+
+    def pass_on(part):
+        for hop, (bit, held) in enumerate(hops):
+            along_copy(hop, part).wait_recv()
+            send_on(held + bit, part)
+
+    for part in range(PARTS + 2):
+        if part < PARTS:
+            for i in range(part * groups, (part + 1) * groups):
+                add_pair(i)
+        if 0 < part <= PARTS:
+            finish_part(part - 1)
+        if part > 1:
+            pass_on(part - 2)
     own_copy = pltpu.make_async_copy(update, updates.at[me], keep)
     own_copy.start()
-    for hop, (bit, held) in enumerate(hops):
-        for part in range(PARTS):
-            along_copy(hop, part).wait_recv()
-            send_on(held + bit, part)
     own_copy.wait()
     for part in range(PARTS):
         for hop in range(len(hops)):
@@ -504,27 +536,48 @@
     )(codes.reshape(replicas, fragment, width), scales.reshape(replicas, fragment, BLOCK), outer_momentum)
 
 
+def outer_kernel(weight, update, new_weight):
+    new_weight[...] = weight[...] - outer_rate * update[0].astype(jnp.float32)
+
+
+def outer_step(weight, updates):
+    replicas, fragment, width = updates.shape
+    rows = pl.BlockSpec((fragment, width), lambda step: (step, 0))
+    return pl.pallas_call(
+        outer_kernel,
+        grid=(replicas,),
+        out_shape=jax.ShapeDtypeStruct(weight.shape, jnp.float32),
+        in_specs=[rows, pl.BlockSpec((1, fragment, width), lambda step: (step, 0, 0))],
+        out_specs=rows,
+        compiler_params=pltpu.CompilerParams(vmem_limit_bytes=32 * 2**20),
+    )(weight, updates)
+
+
 def shards(weight, first_moment, second_moment, outer_momentum, act_table, token_ids, targets):
     row_count, width = weight.shape
     replicas = lax.axis_size("replica")
     fragment = row_count // replicas
     whole_tiles = fragment % TILE == 0 and width % (2 * BLOCK * PARTS) == 0 and width // BLOCK <= BLOCK
-    if not whole_tiles or replicas < 4 or replicas & (replicas - 1):
+    devices = lax.axis_size("mp")
+    if not whole_tiles or replicas < 4 or replicas & (replicas - 1) or devices & (devices - 1):
         return shards_plain(
             weight, first_moment, second_moment, outer_momentum, act_table, token_ids, targets
         )
     wanted = jnp.swapaxes(targets[0], 1, 2)
-    inputs = [
-        lax.all_gather(
-            jnp.take(act_table, token_ids[0, step], axis=0, mode="clip"), "mp", axis=1, tiled=True
-        )
-        for step in range(STEPS)
-    ]
-    current, first, second = first_step(inputs[0], weight, first_moment[0], second_moment[0], wanted[0])
-    codes, scales = second_step(inputs[1], weight, current, first, second, wanted[1])
+    order, bit = [0], devices // 2
+    inputs = [[jnp.take(act_table, token_ids[0, step], axis=0, mode="clip")] for step in range(STEPS)]
+    while bit:
+        to_other = [(device, device ^ bit) for device in range(devices)]
+        order += [held + bit for held in order]
+        inputs = [pieces + [lax.ppermute(piece, "mp", to_other) for piece in pieces] for pieces in inputs]
+        bit //= 2
+    places = lax.axis_index("mp") ^ jnp.array(order, jnp.int32)
+    current, first, second = first_step(
+        places, inputs[0], weight, first_moment[0], second_moment[0], wanted[0]
+    )
+    codes, scales = second_step(places, inputs[1], weight, current, first, second, wanted[1])
     momentum, updates = exchange(codes, scales, outer_momentum, replicas)
-    update = updates.reshape(row_count, width).astype(jnp.float32)
-    return (weight - outer_rate * update, momentum)
+    return (outer_step(weight, updates), momentum)
 
 
 def solution(mesh):

time: 341 us -> 316 us (0.927)
  other arithmetic: 21 us -> 0.55 us
  between operations: 14.1 us -> 0.72 us
  waiting for transfers between devices: 39.6 us -> 49 us
  Pallas kernels: 244 us -> 238 us
  starting transfers between devices: 0.26 us -> 3.95 us
    ppermute x0 -> x6, waiting for transfers between devices: none -> 49 us  [shards(): lax.ppermute(piece, 'mp', to_other)]
    all_gather x2 -> x0, waiting for transfers between devices: 39.5 us -> none  [shards(): lax.all_gather(jnp.take(act_table, token_ids[0, step], axis=0, mode='clip...]
    sub x1 -> x0, other arithmetic: 14.5 us -> none  [shards(): return (weight - outer_rate * update, momentum)]
    pallas_call x1, Pallas kernels: 163 us -> 153 us  [exchange(): pl.pallas_call(functools.partial(exchange_kernel, replicas), out_shape=(j...]
    mul x1 -> x0, other arithmetic: 6.49 us -> none  [shards(): return (weight - outer_rate * update, momentum)]
    pallas_call x0 -> x1, Pallas kernels: none -> 5.9 us  [outer_step(): pl.pallas_call(outer_kernel, grid=(replicas,), out_shape=jax.ShapeDtypeSt...]
    ppermute x0 -> x6, starting transfers between devices: none -> 3.95 us  [shards(): lax.ppermute(piece, 'mp', to_other)]
    unnamed x10 -> x12, local copies, waits for them, and re-layouts: 6.8 us -> 8.42 us
  transfers between devices with their start and end apart: 2 -> 6, of which waited for: 2 -> 2; matrix products, arithmetic and copies ran while one was open for 2% -> 3% of each run, Pallas kernels for 10% -> 11%
where the time goes in v3:
time: 316 us
  Pallas kernels  238 us (75%)
  waiting for transfers between devices  49 us (16%)
  local copies, waits for them, and re-layouts  23.7 us (8%)
  starting transfers between devices  3.95 us (1%)
    pallas_call x1, Pallas kernels, exchange(): pl.pallas_call(functools.partial(exchange_kernel, replicas), out_shape=(j...  153 us
    ppermute x6, waiting for transfers between devices, shards(): lax.ppermute(piece, 'mp', to_other)  49 us
    pallas_call x1, Pallas kernels, second_step(): pl.pallas_call(functools.partial(second_kernel, chunks, factor, factor /...  44.6 us
    pallas_call x1, Pallas kernels, first_step(): pl.pallas_call(functools.partial(first_kernel, chunks, factor, factor / t...  34.6 us
    gather x2, local copies, waits for them, and re-layouts, shards(): jnp.take(act_table, token_ids[0, step], axis=0, mode='clip')  13.3 us
    unnamed x12, local copies, waits for them, and re-layouts  8.42 us
  transfers between devices with their start and end apart: 6, of which 2 were waited for; matrix products, arithmetic and copies ran while one was open for 3% of the time, Pallas kernels for 11%

profile of v3, /device:TPU:0, one launch (start us, length us, event | category | flops | bytes accessed | tf_op | source)
XLA Modules:
  0.0 315.9 jit_solution(4348574107368098681)
XLA Ops:
  0.6 0.8 fusion
  1.4 6.3 %gather_fusion.1 = bf16[512,1280]{1,0:T(8,128)(2,1)S(1)} fusion(bf16[2048,1280]{1,0:T(8,128)(2,1)} %param.12, s32[1024]{0:T(1024)S(1)} %pad_clamp_fusion), kind=kCustom, calls=%fused_computation.1 | custom fusion | bytes 2623488 | tf_op jit(solution)/shard_map/jit(_take)/gather | solution.py:568
  7.7 0.0 copy-start.3
  7.7 3.0 collective-permute-start.3
  10.7 7.1 %gather_fusion = bf16[512,1280]{1,0:T(8,128)(2,1)} fusion(bf16[2048,1280]{1,0:T(8,128)(2,1)} %param.12, s32[1024]{0:T(1024)S(1)} %pad_clamp_fusion.1), kind=kCustom, calls=%fused_computation | custom fusion | bytes 2623488 | tf_op jit(solution)/shard_map/jit(_take)/gather | solution.py:568
  17.8 0.4 collective-permute-start
  18.2 0.0 copy-done.3
  18.2 0.0 collective-permute-start.4
  18.2 22.2 %collective-permute-done.3.refs_1_ = bf16[512,1280]{1,0:T(8,128)(2,1)} collective-permute-done((bf16[512,1280]{1,0:T(8,128)(2,1)S(1)}, bf16[512,1280]{1,0:T(8,128)(2,1)}, u32[]{:S(2)}, u32[]{:S(2)}) %collective-permute-start.3) | collective-permute-done | bytes 1310752 | tf_op jit(solution)/shard_map/ppermute | solution.py:572
  40.4 0.0 collective-permute-start.5
  40.5 0.5 collective-permute-start.1
  41.0 26.7 %collective-permute-done.refs_1_ = bf16[512,1280]{1,0:T(8,128)(2,1)} collective-permute-done((bf16[512,1280]{1,0:T(8,128)(2,1)}, bf16[512,1280]{1,0:T(8,128)(2,1)}, u32[]{:S(2)}, u32[]{:S(2)}) %collective-permute-start) | collective-permute-done | bytes 1310752 | tf_op jit(solution)/shard_map/ppermute | solution.py:572
  67.7 0.0 collective-permute-start.2
  67.7 0.0 copy-start.4
  67.7 1.6 copy.10
  69.3 0.0 copy-done.4
  69.3 0.5 broadcast_xor_fusion.places
  69.9 1.1 slice_bitcast_fusion
  71.0 0.0 collective-permute-done.4.refs_2_
  71.0 0.0 collective-permute-done.5.refs_3_
  71.0 34.6 %shard_map.95 = (f32[640,5120]{1,0:T(8,128)}, f32[640,5120]{1,0:T(8,128)}, f32[640,5120]{1,0:T(8,128)}) custom-call(s32[4]{0:T(128)} %broadcast_xor_fusion.places, bf16[512,1280]{1,0:T(8,128)(2,1)} %copy-done.3, bf16[512,1280]{1,0:T(8,128)(2,1)} %collective-permute-done.3.refs_1_, bf16[512,1280]{1,0:T(8,128)(2,1)} %collective-permute-done.4.refs_2_, ...), custom_call_target="tpu_custom_call" | custom-call | flops 6710886400 | bytes 78643200 | tf_op jit(solution)/shard_map/pallas_call | solution.py:242
  105.6 0.0 collective-permute-done.1.refs_2_
  105.6 0.0 collective-permute-done.2.refs_3_
  105.6 0.0 copy-start.1
  105.7 44.6 %shard_map.96 = (bf16[640,5120]{1,0:T(8,128)(2,1)}, bf16[640,128]{1,0:T(8,128)(2,1)}) custom-call(s32[4]{0:T(128)} %broadcast_xor_fusion.places, bf16[512,1280]{1,0:T(8,128)(2,1)} %gather_fusion, bf16[512,1280]{1,0:T(8,128)(2,1)} %collective-permute-done.refs_1_, bf16[512,1280]{1,0:T(8,128)(2,1)} %collective-permute-done.1.refs_2_, ...), custom_call_target="tpu_custom_call" | custom-call | flops 6710886400 | bytes 72089600 | tf_op jit(solution)/shard_map/pallas_call | solution.py:279
  150.3 0.0 copy-done.1
  150.3 0.0 copy-start.2
  150.3 0.9 copy-done.2
  151.2 153.0 %shard_map.97 = (f32[80,5120]{1,0:T(8,128)S(1)}, bf16[8,80,5120]{2,1,0:T(8,128)(2,1)S(1)}) custom-call(bf16[8,80,5120]{2,1,0:T(8,128)(2,1)} %bitcast.16, bf16[8,80,128]{2,1,0:T(8,128)(2,1)S(1)} %bitcast.13, f32[80,5120]{1,0:T(8,128)S(1)} %copy-done.1), custom_call_target="tpu_custom_call" | custom-call | tf_op jit(solution)/shard_map/pallas_call | solution.py:506
  304.1 0.0 copy-start
  304.2 4.7 %copy-done = f32[640,5120]{1,0:T(8,128)S(1)} copy-done((f32[640,5120]{1,0:T(8,128)S(1)}, f32[640,5120]{1,0:T(8,128)}, u32[]{:S(2)}) %copy-start) | copy-done | bytes 13107224
  308.9 5.9 %shard_map.98 = f32[640,5120]{1,0:T(8,128)} custom-call(f32[640,5120]{1,0:T(8,128)S(1)} %copy-done, bf16[8,80,5120]{2,1,0:T(8,128)(2,1)S(1)} %get-tuple-element.14.update), custom_call_target="tpu_custom_call" | custom-call | tf_op jit(solution)/shard_map/pallas_call | solution.py:546
  314.8 1.2 copy.12
  (2 shorter events, 0.0 us)
Async XLA Ops:
  7.7 10.5 %copy-start.3 = (bf16[512,1280]{1,0:T(8,128)(2,1)}, bf16[512,1280]{1,0:T(8,128)(2,1)S(1)}, u32[]{:S(2)}) copy-start(bf16[512,1280]{1,0:T(8,128)(2,1)S(1)} %gather_fusion.1) | copy-start | bytes 3932164
  7.7 32.7 %collective-permute-start.3 = (bf16[512,1280]{1,0:T(8,128)(2,1)S(1)}, bf16[512,1280]{1,0:T(8,128)(2,1)}, u32[]{:S(2)}, u32[]{:S(2)}) collective-permute-start(bf16[512,1280]{1,0:T(8,128)(2,1)S(1)} %gather_fusion.1), channel_id=1, source_target_pairs={{0,16},{8,24},{16,0},{24,8},{1,17},{9,25},{17,1},{25,9},{2,18},{10... | collective-permute-start | bytes 3932168 | tf_op jit(solution)/shard_map/ppermute | solution.py:572
  17.8 49.9 %collective-permute-start = (bf16[512,1280]{1,0:T(8,128)(2,1)}, bf16[512,1280]{1,0:T(8,128)(2,1)}, u32[]{:S(2)}, u32[]{:S(2)}) collective-permute-start(bf16[512,1280]{1,0:T(8,128)(2,1)} %gather_fusion), channel_id=1, source_target_pairs={{0,16},{8,24},{16,0},{24,8},{1,17},{9,25},{17,1},{25,9},{2,18},{10... | collective-permute-start | bytes 3932168 | tf_op jit(solution)/shard_map/ppermute | solution.py:572
  18.2 52.8 %collective-permute-start.4 = (bf16[512,1280]{1,0:T(8,128)(2,1)S(1)}, bf16[512,1280]{1,0:T(8,128)(2,1)}, u32[]{:S(2)}, u32[]{:S(2)}) collective-permute-start(bf16[512,1280]{1,0:T(8,128)(2,1)S(1)} %gather_fusion.1), channel_id=1, source_target_pairs={{0,8},{8,0},{16,24},{24,16},{1,9},{9,1},{17,25},{25,17},{2,10},{10... | collective-permute-start | bytes 3932168 | tf_op jit(solution)/shard_map/ppermute | solution.py:572
  40.4 30.6 %collective-permute-start.5 = (bf16[512,1280]{1,0:T(8,128)(2,1)}, bf16[512,1280]{1,0:T(8,128)(2,1)}, u32[]{:S(2)}, u32[]{:S(2)}) collective-permute-start(bf16[512,1280]{1,0:T(8,128)(2,1)} %collective-permute-done.3.refs_1_), channel_id=1, source_target_pairs={{0,8},{8,0},{16,24},{24,16},{1,9},{9,1},{17,25},{25,17},{2,10},{10... | collective-permute-start | bytes 3932168 | tf_op jit(solution)/shard_map/ppermute | solution.py:572
  40.5 65.2 %collective-permute-start.1 = (bf16[512,1280]{1,0:T(8,128)(2,1)}, bf16[512,1280]{1,0:T(8,128)(2,1)}, u32[]{:S(2)}, u32[]{:S(2)}) collective-permute-start(bf16[512,1280]{1,0:T(8,128)(2,1)} %gather_fusion), channel_id=1, source_target_pairs={{0,8},{8,0},{16,24},{24,16},{1,9},{9,1},{17,25},{25,17},{2,10},{10... | collective-permute-start | bytes 3932168 | tf_op jit(solution)/shard_map/ppermute | solution.py:572
  67.7 37.9 %collective-permute-start.2 = (bf16[512,1280]{1,0:T(8,128)(2,1)}, bf16[512,1280]{1,0:T(8,128)(2,1)}, u32[]{:S(2)}, u32[]{:S(2)}) collective-permute-start(bf16[512,1280]{1,0:T(8,128)(2,1)} %collective-permute-done.refs_1_), channel_id=1, source_target_pairs={{0,8},{8,0},{16,24},{24,16},{1,9},{9,1},{17,25},{25,17},{2,10},{10... | collective-permute-start | bytes 3932168 | tf_op jit(solution)/shard_map/ppermute | solution.py:572
  67.7 1.6 copy-start.4
  105.6 44.6 %copy-start.1 = (f32[80,5120]{1,0:T(8,128)S(1)}, f32[80,5120]{1,0:T(8,128)}, u32[]{:S(2)}) copy-start(f32[80,5120]{1,0:T(8,128)} %outer.1) | copy-start | bytes 4915204
  150.3 0.9 copy-start.2
  304.1 4.7 %copy-start = (f32[640,5120]{1,0:T(8,128)S(1)}, f32[640,5120]{1,0:T(8,128)}, u32[]{:S(2)}) copy-start(f32[640,5120]{1,0:T(8,128)} %weight.1) | copy-start | bytes 39321604
